TPU v7x, 256 devices: a whole 4x4x8 slice. The times are simulated.
256 devices in a mesh: replica: 4 (over z_lo, core), fsdp: 64 (over z_hi, y, x).
Axes of the slice: x: 4, y: 4, z: 8 (z_hi: 4, z_lo: 2; z = z_hi * 2 + z_lo), core: 2. Of those that a mesh axis runs over, the one named last changes fastest.
Arguments:
- outer_gate: float32 [4096, 16384], P('replica', 'fsdp'), may hold values from -6 to 6
- outer_up: float32 [4096, 16384], P('replica', 'fsdp'), may hold values from -6 to 6
- outer_down: float32 [4096, 16384], P('replica', 'fsdp'), may hold values from -6 to 6
- momentum_gate: float32 [4096, 16384], P('replica', 'fsdp'), may hold values from -0.75 to 0.75
- momentum_up: float32 [4096, 16384], P('replica', 'fsdp'), may hold values from -0.75 to 0.75
- momentum_down: float32 [4096, 16384], P('replica', 'fsdp'), may hold values from -0.75 to 0.75
- inputs: bfloat16 [2, 4, 256, 4096], P(None, 'replica', 'fsdp'), may hold values from -6 to 6
- targets: bfloat16 [2, 4, 256, 4096], P(None, 'replica', 'fsdp'), may hold values from -6 to 6
- loss_flags: int32 [2, 4, 256], P(None, 'replica', 'fsdp'), may hold values 0 or 1
Outputs:
- new_gate: float32 [4096, 16384], P('replica', 'fsdp')
- new_up: float32 [4096, 16384], P('replica', 'fsdp')
- new_down: float32 [4096, 16384], P('replica', 'fsdp')
- new_momentum_gate: float32 [4096, 16384], P('replica', 'fsdp')
- new_momentum_up: float32 [4096, 16384], P('replica', 'fsdp')
- new_momentum_down: float32 [4096, 16384], P('replica', 'fsdp')
All inputs are finite; a program needn't handle non-finite values. No bound on the sum of `loss_flags` on one device may be relied on, other than what follows from the above.
Results may differ from a plain program's by a relative error of at most 0.012.
Values may be sent and summed in bfloat16 or wider, within the bound.
No kernel may reach another device: no remote copies, remote signals or barrier semaphores. Data moves between devices by JAX's collectives and lax.ppermute only.
A program may use at most 128 MiB of HBM per device.

v0:
```python
import math

import jax
import jax.numpy as jnp
from jax import lax
from jax.sharding import PartitionSpec as P

D = 4096
FF = 16384
ITERS = 2


BETA_ONE = 0.9
BETA_TWO = 0.95
INNER_RATE = 0.05
DECAY_RATE = 0.1
OUTER_RATE = 0.7
MOMENTUM_RATE = 0.9


def contract_rows(left, right):
    return lax.dot_general(
        left, right, (((0,), (0,)), ((), ())), preferred_element_type=jnp.float32
    )


def contract_cols(left, right):
    return lax.dot_general(
        left, right, (((1,), (1,)), ((), ())), preferred_element_type=jnp.float32
    )


def adamw_update(weight, moment, second, grad, count, epsilon):
    moment = BETA_ONE * moment + (1.0 - BETA_ONE) * grad
    second = BETA_TWO * second + (1.0 - BETA_TWO) * grad * grad
    first_hat = moment / (1.0 - BETA_ONE**count)
    second_hat = second / (1.0 - BETA_TWO**count)
    weight = weight - INNER_RATE * (
        first_hat / (jnp.sqrt(second_hat) + epsilon) + DECAY_RATE * weight
    )
    return (weight, moment, second)


def per_device(
    outer_gate,
    outer_up,
    outer_down,
    momentum_gate,
    momentum_up,
    momentum_down,
    inputs,
    targets,
    loss_flags,
):
    local_rows = inputs.shape[2]
    total_rows = local_rows * lax.axis_size("fsdp")
    scale_in = D ** (-0.5)
    scale_hidden = FF ** (-0.5)
    epsilon = 1.0 / math.sqrt(FF * total_rows)
    outer_full = (
        lax.all_gather(outer_gate.astype(jnp.bfloat16), "replica", axis=0, tiled=True).astype(
            outer_gate.dtype
        ),
        lax.all_gather(outer_up.astype(jnp.bfloat16), "replica", axis=0, tiled=True).astype(
            outer_up.dtype
        ),
        lax.all_gather(outer_down.astype(jnp.bfloat16), "replica", axis=0, tiled=True).astype(
            outer_down.dtype
        ),
    )
    weights = list(outer_full)
    moments = [jnp.zeros_like(item) for item in outer_full]
    seconds = [jnp.zeros_like(item) for item in outer_full]
    for step in range(ITERS):
        batch = lax.all_gather(inputs[step, 0], "fsdp", axis=0, tiled=True)
        w_gate, w_up, w_down = [item.astype(jnp.bfloat16) for item in weights]
        gate_pre = jnp.dot(batch, w_gate, preferred_element_type=jnp.float32) * scale_in
        up_pre = jnp.dot(batch, w_up, preferred_element_type=jnp.float32) * scale_in
        sigma = jax.nn.sigmoid(gate_pre)
        active = gate_pre * sigma
        hidden = (active * up_pre).astype(jnp.bfloat16)
        output = lax.psum_scatter(
            contract_cols(hidden, w_down) * scale_hidden, "fsdp", scatter_dimension=0, tiled=True
        )
        flags_own = loss_flags[step, 0].astype(jnp.float32)
        own_grad = (
            flags_own[:, None] * (output - targets[step, 0].astype(jnp.float32)) / total_rows
        ).astype(jnp.bfloat16)
        out_grad = lax.all_gather(own_grad, "fsdp", axis=0, tiled=True)
        grad_down = contract_rows(out_grad, hidden) * scale_hidden
        hidden_grad = jnp.dot(out_grad, w_down, preferred_element_type=jnp.float32) * scale_hidden
        gate_grad = (hidden_grad * up_pre * sigma * (1.0 + gate_pre * (1.0 - sigma))).astype(
            jnp.bfloat16
        )
        up_grad = (hidden_grad * active).astype(jnp.bfloat16)
        grad_gate = contract_rows(batch, gate_grad) * scale_in
        grad_up = contract_rows(batch, up_grad) * scale_in
        grads = (grad_gate, grad_up, grad_down)
        for index in range(3):
            weights[index], moments[index], seconds[index] = adamw_update(
                weights[index], moments[index], seconds[index], grads[index], step + 1, epsilon
            )
    deltas = tuple((outer_full[index] - weights[index] for index in range(3)))
    summed = (
        lax.psum_scatter(
            deltas[0].astype(jnp.bfloat16), "replica", scatter_dimension=0, tiled=True
        ).astype(jnp.float32),
        lax.psum_scatter(
            deltas[1].astype(jnp.bfloat16), "replica", scatter_dimension=0, tiled=True
        ).astype(jnp.float32),
        lax.psum_scatter(
            deltas[2].astype(jnp.bfloat16), "replica", scatter_dimension=0, tiled=True
        ).astype(jnp.float32),
    )
    outer_own = (outer_gate, outer_up, outer_down)
    momenta = (momentum_gate, momentum_up, momentum_down)
    replicas = lax.axis_size("replica")
    new_params = []
    new_momenta = []
    for index in range(3):
        average = summed[index] / replicas
        fresh = MOMENTUM_RATE * momenta[index] + average
        new_momenta.append(fresh)
        new_params.append(outer_own[index] - OUTER_RATE * (average + MOMENTUM_RATE * fresh))
    return (
        new_params[0],
        new_params[1],
        new_params[2],
        new_momenta[0],
        new_momenta[1],
        new_momenta[2],
    )


def solution(mesh):
    in_specs = (
        P("replica", "fsdp"),
        P("replica", "fsdp"),
        P("replica", "fsdp"),
        P("replica", "fsdp"),
        P("replica", "fsdp"),
        P("replica", "fsdp"),
        P(None, "replica", "fsdp", None),
        P(None, "replica", "fsdp", None),
        P(None, "replica", "fsdp"),
    )
    out_specs = (
        P("replica", "fsdp"),
        P("replica", "fsdp"),
        P("replica", "fsdp"),
        P("replica", "fsdp"),
        P("replica", "fsdp"),
        P("replica", "fsdp"),
    )
    return jax.shard_map(
        per_device, mesh=mesh, in_specs=in_specs, out_specs=out_specs, check_vma=False
    )
```

profile of v0, /device:TPU:1, one launch (start us, length us, event | category | flops | bytes accessed | tf_op | source)
XLA Modules:
  0.0 2109.3 jit_solution(7149756971760640553)
XLA Ops:
  16.1 88.8 %all-gather.18.cloned.1.call-done = bf16[1,1,256,4096]{3,1,0,2:T(2,128)(2,1)} async-done(((bf16[1,1,4,4096]{3,1,0,2:T(2,128)(2,1)}), bf16[1,1,256,4096]{3,1,0,2:T(2,128)(2,1)}) %all-gather.18.cloned.1.call-update) | async-done | bytes 2097168 | tf_op jit(solution)/shard_map/all_gather | solution.py:75
  104.9 4.5 copy.115
  109.4 28.5 %all-gather.12.cloned.1.call-done = bf16[4096,256]{0,1:T(8,128)(2,1)} async-done(((bf16[1024,256]{0,1:T(8,128)(2,1)}), bf16[4096,256]{0,1:T(8,128)(2,1)}) %all-gather.12.cloned.1.call-update) | async-done | bytes 2097168 | tf_op jit(solution)/shard_map/all_gather | solution.py:61
  143.6 28.8 %all-gather.14.cloned.1.call-done = bf16[4096,256]{0,1:T(8,128)(2,1)} async-done(((bf16[1024,256]{0,1:T(8,128)(2,1)}), bf16[4096,256]{0,1:T(8,128)(2,1)}) %all-gather.14.cloned.1.call-update) | async-done | bytes 2097168 | tf_op jit(solution)/shard_map/all_gather | solution.py:64
  172.4 3.1 multiply_convert_fusion.5
  175.5 31.2 %all-gather.16.cloned.1.call-done = bf16[4096,256]{0,1:T(8,128)(2,1)} async-done(((bf16[1024,256]{0,1:T(8,128)(2,1)}), bf16[4096,256]{0,1:T(8,128)(2,1)}) %all-gather.16.cloned.1.call-update) | async-done | bytes 2097168 | tf_op jit(solution)/shard_map/all_gather | solution.py:67
  206.7 4.4 convolution_multiply_fusion.1
  213.8 702.5 %all-reduce.5.cloned.1.call-done = f32[256,4096]{1,0:T(8,128)} async-done(((f32[256,4096]{1,0:T(8,128)}), f32[256,4096]{1,0:T(8,128)}) %all-reduce.5.cloned.1.call-update) | async-done | bytes 4194320
  918.0 131.9 %all-gather.20.cloned.1.call-done = bf16[1,1,256,4096]{3,1,0,2:T(2,128)(2,1)} async-done(((bf16[1,1,4,4096]{3,1,0,2:T(2,128)(2,1)}), bf16[1,1,256,4096]{3,1,0,2:T(2,128)(2,1)}) %all-gather.20.cloned.1.call-update) | async-done | bytes 2097168 | tf_op jit(solution)/shard_map/all_gather | solution.py:75
  1049.8 5.9 copy.116
  1055.8 73.4 %all-gather.22.cloned.1.call-done = bf16[64,4,4096]{2,1,0:T(4,128)(2,1)} async-done(((bf16[1,4,4096]{2,1,0:T(4,128)(2,1)}), bf16[64,4,4096]{2,1,0:T(4,128)(2,1)}) %all-gather.22.cloned.1.call-update) | async-done | bytes 2097168 | tf_op jit(solution)/shard_map/all_gather | solution.py:89
  1129.1 4.5 reshape.33
  1133.6 3.7 fusion.100
  1143.8 5.0 fusion.45
  1151.8 3.7 multiply_convert_fusion.2
  1158.4 703.4 %all-reduce.7.cloned.1.call-done = f32[256,4096]{1,0:T(8,128)} async-done(((f32[256,4096]{1,0:T(8,128)}), f32[256,4096]{1,0:T(8,128)}) %all-reduce.7.cloned.1.call-update) | async-done | bytes 4194320
  1863.5 120.0 %all-gather.24.cloned.1.call-done = bf16[64,4,4096]{2,1,0:T(4,128)(2,1)} async-done(((bf16[1,4,4096]{2,1,0:T(4,128)(2,1)}), bf16[64,4,4096]{2,1,0:T(4,128)(2,1)}) %all-gather.24.cloned.1.call-update) | async-done | bytes 2097168 | tf_op jit(solution)/shard_map/all_gather | solution.py:89
  1983.6 4.0 reshape.35
  1987.5 10.1 fusion.8
  1997.7 3.1 convolution_multiply_fusion.2
  2001.7 9.0 fusion.5
  2011.0 9.8 fusion.2
  2036.5 25.9 %reduce-scatter.6.cloned.1.call-done = bf16[1024,256]{0,1:T(8,128)(2,1)} async-done(((bf16[4096,256]{0,1:T(8,128)(2,1)}), bf16[1024,256]{0,1:T(8,128)(2,1)}) %reduce-scatter.6.cloned.1.call-update) | async-done | bytes 524304 | tf_op jit(solution)/shard_map/reduce_scatter | solution.py:108
  2070.5 25.6 %reduce-scatter.4.cloned.1.call-done = bf16[1024,256]{0,1:T(8,128)(2,1)} async-done(((bf16[4096,256]{0,1:T(8,128)(2,1)}), bf16[1024,256]{0,1:T(8,128)(2,1)}) %reduce-scatter.4.cloned.1.call-update) | async-done | bytes 524304 | tf_op jit(solution)/shard_map/reduce_scatter | solution.py:105
  (112 shorter events, 63.4 us)
Async XLA Ops:
  7.2 97.7 %all-gather.18.cloned.1.call-start = ((), (), s32[]{:S(2)}) async-start(), calls=%async_computation.9 | async-start | bytes 4259840 | tf_op jit(solution)/shard_map/all_gather | solution.py:75
  9.4 128.5 %all-gather.12.cloned.1.call-start = ((), (), s32[]{:S(2)}) async-start(), calls=%async_computation.3 | async-start | bytes 2621440 | tf_op jit(solution)/shard_map/all_gather | solution.py:61
  11.9 160.5 %all-gather.14.cloned.1.call-start = ((), (), s32[]{:S(2)}) async-start(), calls=%async_computation.4 | async-start | bytes 2621440 | tf_op jit(solution)/shard_map/all_gather | solution.py:64
  13.4 193.3 %all-gather.16.cloned.1.call-start = ((), (), s32[]{:S(2)}) async-start(), calls=%async_computation.5 | async-start | bytes 2621440 | tf_op jit(solution)/shard_map/all_gather | solution.py:67
  16.0 900.3 %all-reduce.5.cloned.1.call-start = ((), (), s32[]{:S(2)}) async-start(), calls=%async_computation.13 | async-start | bytes 8388608
  141.0 70.1 %copy-start.18 = (f32[256,256]{1,0:T(8,128)}, f32[256,256]{1,0:T(8,128)S(1)}, u32[]{:S(2)}) copy-start(f32[256,256]{1,0:T(8,128)S(1)} %get-tuple-element.37) | copy-start | bytes 786436
  206.7 5.9 copy-start.25
  206.7 7.1 copy-start.23
  211.1 705.2 %copy-start.21 = (bf16[2,1,4,4096]{3,2,1,0:T(4,128)(2,1)S(1)}, bf16[2,1,4,4096]{3,2,1,0:T(4,128)(2,1)}, u32[]{:S(2)}) copy-start(bf16[2,1,4,4096]{3,2,1,0:T(4,128)(2,1)} %param.16) | copy-start | bytes 196612
  211.1 838.7 %all-gather.20.cloned.1.call-start = ((), (), s32[]{:S(2)}) async-start(), calls=%async_computation.10 | async-start | bytes 4259840 | tf_op jit(solution)/shard_map/all_gather | solution.py:75
  212.6 916.6 %all-gather.22.cloned.1.call-start = ((), (), s32[]{:S(2)}) async-start(), calls=%async_computation.11 | async-start | bytes 2129920 | tf_op jit(solution)/shard_map/all_gather | solution.py:89
  917.9 943.9 %all-reduce.7.cloned.1.call-start = ((), (), s32[]{:S(2)}) async-start(), calls=%async_computation.14 | async-start | bytes 8388608
  1140.0 8.8 copy-start.7
  1143.7 8.0 copy-start.8
  1148.8 6.7 copy-start.13
  1155.5 706.4 %copy-start.22 = (bf16[2,1,4,4096]{3,2,1,0:T(4,128)(2,1)S(1)}, bf16[2,1,4,4096]{3,2,1,0:T(4,128)(2,1)}, u32[]{:S(2)}) copy-start(bf16[2,1,4,4096]{3,2,1,0:T(4,128)(2,1)} %param.16) | copy-start | bytes 196612
  1158.2 829.3 %copy-start.5 = (bf16[4096,256]{0,1:T(8,128)(2,1)S(1)}, bf16[4096,256]{0,1:T(8,128)(2,1)}, u32[]{:S(2)}) copy-start(bf16[4096,256]{0,1:T(8,128)(2,1)} %all-gather.16.cloned.1.call-done) | copy-start | bytes 6291460
  1158.2 825.4 %all-gather.24.cloned.1.call-start = ((), (), s32[]{:S(2)}) async-start(), calls=%async_computation.12 | async-start | bytes 2129920 | tf_op jit(solution)/shard_map/all_gather | solution.py:89
  1863.5 164.9 %reduce-scatter.8.cloned.1.call-start = ((), (), s32[]{:S(2)}) async-start(), calls=%async_computation.8 | async-start | bytes 2621440 | tf_op jit(solution)/shard_map/reduce_scatter | solution.py:111
  1997.7 64.7 %reduce-scatter.6.cloned.1.call-start = ((), (), s32[]{:S(2)}) async-start(), calls=%async_computation.7 | async-start | bytes 2621440 | tf_op jit(solution)/shard_map/reduce_scatter | solution.py:108
  2010.8 85.3 %reduce-scatter.4.cloned.1.call-start = ((), (), s32[]{:S(2)}) async-start(), calls=%async_computation.6 | async-start | bytes 2621440 | tf_op jit(solution)/shard_map/reduce_scatter | solution.py:105
  2020.8 7.6 copy-start.3
  2027.4 35.0 %copy-start.1 = (f32[1024,256]{0,1:T(8,128)S(1)}, f32[1024,256]{0,1:T(8,128)}, u32[]{:S(2)}) copy-start(f32[1024,256]{0,1:T(8,128)} %copy-done) | copy-start | bytes 3145732
  2036.5 59.5 %copy-start.10 = (f32[1024,256]{0,1:T(8,128)S(1)}, f32[1024,256]{0,1:T(8,128)}, u32[]{:S(2)}) copy-start(f32[1024,256]{0,1:T(8,128)} %copy.93) | copy-start | bytes 3145732
  (15 other events, 47.8 us)
Sparse Core Ops, SparseCore 0:
  11.9 92.9 all-gather.17
  107.3 30.5 all-gather.11
  140.3 32.0 all-gather.13
  174.6 32.0 all-gather.15
  211.3 704.9 all-reduce.4
  920.6 129.2 all-gather.19
  1053.6 75.4 all-gather.21
  1158.3 703.4 all-reduce.6
  1865.7 117.7 all-gather.23
  1997.8 30.5 reduce-scatter.7
  2031.1 31.2 reduce-scatter.5
  2064.8 31.2 reduce-scatter.3
where the time goes:
time: 2120 us; the launch traced here: 2110 us
  waiting for transfers between devices  1960 us (92%)
  matrix products  63.3 us (3%)
  local copies, waits for them, and re-layouts  54.3 us (3%)
    unnamed x14, waiting for transfers between devices  1410 us
    all_gather x2, waiting for transfers between devices, per_device(): batch = lax.all_gather(inputs[step, 0], 'fsdp', axis=0, tiled=True)  221 us
    all_gather x2, waiting for transfers between devices, per_device(): out_grad = lax.all_gather(own_grad, 'fsdp', axis=0, tiled=True)  193 us
    unnamed x73, local copies, waits for them, and re-layouts  49.4 us
  transfers between devices with their start and end apart: 12, of which 12 were waited for; matrix products, arithmetic and copies ran while one was open for 3% of the time, Pallas kernels for 0%

commit v1 on v0

v1 whole, which is shorter than its diff:
```python
import math

import jax
import jax.numpy as jnp
from jax import lax
from jax.sharding import Mesh, PartitionSpec as P

ITERS = 2
BETA_ONE = 0.9
BETA_TWO = 0.95
INNER_RATE = 0.05
DECAY_RATE = 0.1
OUTER_RATE = 0.7
MOMENTUM_RATE = 0.9

AXES = ("a", "c", "h", "y", "x")
SIZES = (2, 2, 4, 4, 4)
PLANE = ("y", "x")
BF16 = jnp.bfloat16
F32 = jnp.float32


def contract_rows(left, right):
    return lax.dot_general(
        left, right, (((0,), (0,)), ((), ())), preferred_element_type=F32
    )


def contract_cols(left, right):
    return lax.dot_general(
        left, right, (((1,), (1,)), ((), ())), preferred_element_type=F32
    )


def swap_core(value):
    return lax.ppermute(value, "c", ((0, 1), (1, 0)))


def swap_chip(value):
    return lax.ppermute(value, "a", ((0, 1), (1, 0)))


def relative_blocks(value):
    shape = value.shape
    parts = value.reshape(shape[:-1] + (2, 2, shape[-1] // 4))
    core, chip = lax.axis_index("c"), lax.axis_index("a")
    parts = jnp.where(core == 1, parts[..., ::-1, :], parts)
    parts = jnp.where(chip == 1, parts[..., ::-1, :, :], parts)
    return parts.reshape(shape)


def spread_plane(value):
    copies = lax.psum(1, PLANE)
    return lax.all_to_all(
        jnp.broadcast_to(value[None], (copies,) + value.shape), PLANE, 0, 0
    ).reshape((copies * value.shape[0],) + value.shape[1:])


def sum_plane(value):
    copies = lax.psum(1, PLANE)
    parts = value.reshape((copies, value.shape[0] // copies) + value.shape[1:])
    parts = lax.all_to_all(parts, PLANE, 0, 0)
    return jnp.sum(parts.astype(F32), axis=0)


def sum_height(value):
    sent = value.astype(BF16)
    total = value
    for shift in range(1, SIZES[2]):
        pairs = [(i, (i + shift) % SIZES[2]) for i in range(SIZES[2])]
        total = total + lax.ppermute(sent, "h", pairs).astype(F32)
    return total


def per_device(
    outer_gate,
    outer_up,
    outer_down,
    momentum_gate,
    momentum_up,
    momentum_down,
    inputs,
    targets,
    loss_flags,
):
    tokens = inputs.shape[2]
    features = inputs.shape[3]
    total_rows = tokens * 64
    hidden_units = outer_gate.shape[1] * 64
    scale_in = features ** (-0.5)
    scale_hidden = hidden_units ** (-0.5)
    epsilon = 1.0 / math.sqrt(hidden_units * total_rows)

    own_gu = jnp.stack([outer_gate.astype(BF16), outer_up.astype(BF16)])
    own_d = outer_down.astype(BF16)[None]
    far_gu = swap_chip(own_gu)
    far_d = swap_chip(own_d)
    near_gu = swap_core(own_gu)
    near_d = swap_core(own_d)

    flag_row = jnp.zeros((ITERS, 1, features), BF16)
    flag_row = flag_row.at[:, 0, :tokens].set(loss_flags[:, 0].astype(BF16))
    packed = jnp.concatenate(
        [relative_blocks(inputs[:, 0]), relative_blocks(targets[:, 0]), flag_row], axis=1
    )
    column = lax.all_gather(packed, "h", axis=0)
    column = jnp.swapaxes(column, 0, 1)
    x_rows = column[:, :, :tokens].reshape(ITERS, 4 * tokens, features)
    t_rows = column[:, :, tokens : 2 * tokens].reshape(ITERS, 4 * tokens, features)
    flags = column[:, :, 2 * tokens, :tokens].reshape(ITERS, 4 * tokens).astype(F32)

    batch_one = spread_plane(x_rows[0])
    far_near_gu = swap_core(far_gu)
    far_near_d = swap_core(far_d)
    w_gu = jnp.concatenate([own_gu, near_gu, far_gu, far_near_gu], axis=1)
    w_d = jnp.concatenate([own_d, near_d, far_d, far_near_d], axis=1)
    start = (w_gu[0], w_gu[1], w_d[0])
    batch_two = lax.all_gather(x_rows[1], PLANE, axis=0, tiled=True)

    weights = start
    first = None
    deltas = None
    for step in range(ITERS):
        batch = batch_one if step == 0 else batch_two
        w_gate, w_up, w_down = weights
        gate_pre = jnp.dot(batch, w_gate, preferred_element_type=F32) * scale_in
        up_pre = jnp.dot(batch, w_up, preferred_element_type=F32) * scale_in
        sigma = jax.nn.sigmoid(gate_pre)
        active = gate_pre * sigma
        hidden = (active * up_pre).astype(BF16)
        partial = (contract_cols(hidden, w_down) * scale_hidden).astype(BF16)
        output = sum_height(sum_plane(partial))
        own_grad = (
            flags[step][:, None] * (output - t_rows[step].astype(F32)) / total_rows
        ).astype(BF16)
        out_grad = spread_plane(own_grad)
        grad_down = contract_rows(out_grad, hidden) * scale_hidden
        hidden_grad = jnp.dot(out_grad, w_down, preferred_element_type=F32) * scale_hidden
        gate_grad = (
            hidden_grad * up_pre * sigma * (1.0 + gate_pre * (1.0 - sigma))
        ).astype(BF16)
        up_grad = (hidden_grad * active).astype(BF16)
        grad_gate = contract_rows(batch, gate_grad) * scale_in
        grad_up = contract_rows(batch, up_grad) * scale_in
        grads = (grad_gate, grad_up, grad_down)
        keep = 1.0 - INNER_RATE * DECAY_RATE
        if step == 0:
            first = [item.astype(BF16) for item in grads]
            weights = [
                (
                    keep * w.astype(F32) - INNER_RATE * (g / (jnp.abs(g) + epsilon))
                ).astype(BF16)
                for w, g in zip(start, grads)
            ]
        else:
            m_one = BETA_ONE * (1.0 - BETA_ONE) / (1.0 - BETA_ONE**2)
            m_two = (1.0 - BETA_ONE) / (1.0 - BETA_ONE**2)
            v_one = BETA_TWO * (1.0 - BETA_TWO) / (1.0 - BETA_TWO**2)
            v_two = (1.0 - BETA_TWO) / (1.0 - BETA_TWO**2)
            deltas = []
            for w, p, g in zip(start, first, grads):
                p = p.astype(F32)
                u_one = p / (jnp.abs(p) + epsilon)
                u_two = (m_one * p + m_two * g) / (
                    jnp.sqrt(v_one * p * p + v_two * g * g) + epsilon
                )
                deltas.append(
                    (
                        (1.0 - keep * keep) * w.astype(F32)
                        + (keep * INNER_RATE) * u_one
                        + INNER_RATE * u_two
                    ).astype(BF16)
                )

    outer_own = (outer_gate, outer_up, outer_down)
    momenta = (momentum_gate, momentum_up, momentum_down)
    rows = outer_gate.shape[0]
    new_params = [None] * 3
    new_momenta = [None] * 3
    for index in (2, 0, 1):
        delta = deltas[index].reshape(4, rows, -1)
        near = swap_core(jnp.stack([delta[1], delta[3]]))
        far = swap_chip((delta[2].astype(F32) + near[1].astype(F32)).astype(BF16))
        summed = delta[0].astype(F32) + near[0].astype(F32) + far.astype(F32)
        average = summed / 4.0
        fresh = MOMENTUM_RATE * momenta[index] + average
        new_momenta[index] = fresh
        new_params[index] = outer_own[index] - OUTER_RATE * (
            average + MOMENTUM_RATE * fresh
        )
    return tuple(new_params) + tuple(new_momenta)


def solution(mesh):
    fine = Mesh(mesh.devices.reshape(SIZES), AXES)
    rep, fsdp = ("a", "c"), ("h", "y", "x")
    state = P(rep, fsdp)
    rows = P(None, rep, fsdp, None)
    return jax.shard_map(
        per_device,
        mesh=fine,
        in_specs=(state,) * 6 + (rows, rows, P(None, rep, fsdp)),
        out_specs=(state,) * 6,
        check_vma=False,
    )
```

time: 2120 us -> 396 us (0.19)
  waiting for transfers between devices: 1960 us -> 104 us
  blocking collectives: 0 us -> 138 us
  starting transfers between devices: 0.88 us -> 53.6 us
  local copies, waits for them, and re-layouts: 54.3 us -> 8.99 us
    unnamed x14 -> x1, waiting for transfers between devices: 1410 us -> 0.02 us
    all_gather x7 -> x1, waiting for transfers between devices: 503 us -> 22.7 us  [per_device(): batch_two = lax.all_gather(x_rows[1], PLANE, axis=0, tiled=True)]
    all_to_all x0 -> x3, blocking collectives: none -> 96.6 us  [the longest x2 66.2 us: sum_plane(): parts = lax.all_to_all(parts, PLANE, 0, 0)]
    ppermute x0 -> x18, waiting for transfers between devices: none -> 56.2 us  [the longest x5 40.7 us: swap_chip(): return lax.ppermute(value, 'a', ((0, 1), (1, 0)))]
    reduce_scatter x3 -> x0, waiting for transfers between devices: 52.4 us -> none  [the longest x1 25.9 us: per_device(): lax.psum_scatter(deltas[1].astype(jnp.bfloat16), 'replica', scatter_dimen...]
    unnamed x73 -> x52, local copies, waits for them, and re-layouts: 49.4 us -> 2.87 us
    ppermute x0 -> x18, starting transfers between devices: none -> 42.8 us  [the longest x6 21.6 us: sum_height(): total = total + lax.ppermute(sent, 'h', pairs).astype(F32)]
    all_gather x0 -> x1, blocking collectives: none -> 41.9 us  [per_device(): column = lax.all_gather(packed, 'h', axis=0)]
  transfers between devices with their start and end apart: 12 -> 21, of which waited for: 12 -> 11; matrix products, arithmetic and copies ran while one was open for 3% -> 12% of each run, Pallas kernels for 0% -> 0%
where the time goes in v1:
time: 396 us; the launch traced here: 391 us
  blocking collectives  138 us (35%)
  waiting for transfers between devices  104 us (26%)
  starting transfers between devices  53.6 us (14%)
  matrix products  45.3 us (11%)
  other arithmetic  25.2 us (6%)
  between operations  14.8 us (4%)
  local copies, waits for them, and re-layouts  8.99 us (2%)
    all_to_all x2, blocking collectives, sum_plane(): parts = lax.all_to_all(parts, PLANE, 0, 0)  66.2 us
    all_gather x1, blocking collectives, per_device(): column = lax.all_gather(packed, 'h', axis=0)  41.9 us
    ppermute x5, waiting for transfers between devices, swap_chip(): return lax.ppermute(value, 'a', ((0, 1), (1, 0)))  40.7 us
    all_to_all x1, blocking collectives, spread_plane(): lax.all_to_all(jnp.broadcast_to(value[None], (copies,) + value.shape), PL...  30.4 us
    dot_general x6, matrix products, contract_rows(): lax.dot_general(left, right, (((0,), (0,)), ((), ())), preferred_element_...  27.6 us
    all_to_all x2, waiting for transfers between devices, spread_plane(): lax.all_to_all(jnp.broadcast_to(value[None], (copies,) + value.shape), PL...  25.4 us
    all_gather x1, waiting for transfers between devices, per_device(): batch_two = lax.all_gather(x_rows[1], PLANE, axis=0, tiled=True)  22.7 us
    ppermute x6, starting transfers between devices, sum_height(): total = total + lax.ppermute(sent, 'h', pairs).astype(F32)  21.6 us
  transfers between devices with their start and end apart: 21, of which 11 were waited for; matrix products, arithmetic and copies ran while one was open for 12% of the time, Pallas kernels for 0%

profile of v1, /device:TPU:1, one launch (start us, length us, event | category | flops | bytes accessed | tf_op | source)
XLA Modules:
  0.0 390.7 jit_solution(12187396443734750296)
XLA Ops:
  14.2 41.9 %all-gather = bf16[8,9,4096]{2,1,0:T(8,128)(2,1)S(1)} all-gather(bf16[2,9,4096]{2,1,0:T(8,128)(2,1)S(1)} %fusion.65), channel_id=2, replica_groups=mesh['a'=2,'c'=2,'h'=4,'y'=4,'x'=4] {'h'}, dimensions={0}, use_global_device_ids=true | all-gather | bytes 737280 | tf_op jit(solution)/shard_map/all_gather | solution.py:106
  59.6 6.4 %all-to-all-start = ((bf16[16,16,4096]{2,1,0:T(8,128)(2,1)}), bf16[16,16,4096]{2,1,0:T(8,128)(2,1)S(1)}, u32[]{:S(2)}, u32[]{:S(2)}) async-start(bf16[16,16,4096]{2,1,0:T(8,128)(2,1)} %broadcast_in_dim.11), calls=%async_computation | async-start | bytes 4194304 | tf_op jit(solution)/shard_map/all_to_all | solution.py:54
  73.8 11.5 %collective-permute-done.4 = bf16[1,1024,256]{2,1,0:T(8,128)(2,1)} collective-permute-done((bf16[1,1024,256]{2,1,0:T(8,128)(2,1)}, bf16[1,1024,256]{2,1,0:T(8,128)(2,1)}, u32[]{:S(2)}, u32[]{:S(2)}) %collective-permute-start.4) | collective-permute-done | bytes 524320 | tf_op jit(solution)/shard_map/ppermute | solution.py:40
  86.6 10.0 %pad_maximum_fusion = bf16[2,4096,256]{2,1,0:T(8,128)(2,1)} fusion(bf16[2,1024,256]{2,1,0:T(8,128)(2,1)S(1)} %collective-permute-done.2, bf16[2,1024,256]{2,1,0:T(8,128)(2,1)} %collective-permute-done.1, bf16[2,1024,256]{2,1,0:T(8,128)(2,1)S(1)} %collective-permute-done, bf16[1,1024,256]{2,1,0:T(8,128)(2,1)S(1)} %get-tuple-element.44, ...), kind=kLoop, calls=%fused_computation.67 | loop fusion | flops 20971520 | bytes 8388608 | tf_op jit(solution)/shard_map/concatenate | solution.py:115
  103.2 34.8 %all_to_all.25 = bf16[16,16,4096]{2,1,0:T(8,128)(2,1)S(1)} all-to-all(bf16[16,16,4096]{2,1,0:T(8,128)(2,1)S(1)} %bitcast.130), channel_id=1, replica_groups=mesh['a'=2,'c'=2,'h'=4,'y'=4,'x'=4] {'y','x'}, dimensions={0} | all-to-all | bytes 4194304 | tf_op jit(solution)/shard_map/all_to_all | solution.py:62
  145.7 4.9 %collective-permute-done.7 = bf16[16,4096]{1,0:T(8,128)(2,1)} collective-permute-done((bf16[16,4096]{1,0:T(8,128)(2,1)}, bf16[16,4096]{1,0:T(8,128)(2,1)}, u32[]{:S(2)}, u32[]{:S(2)}) %collective-permute-start.7) | collective-permute-done | bytes 131104 | tf_op jit(solution)/shard_map/ppermute | solution.py:71
  155.6 4.4 %all-to-all-start.2 = ((bf16[16,16,4096]{2,1,0:T(8,128)(2,1)}), bf16[16,16,4096]{2,1,0:T(8,128)(2,1)}, u32[]{:S(2)}, u32[]{:S(2)}) async-start(bf16[16,16,4096]{2,1,0:T(8,128)(2,1)} %broadcast_in_dim.26), calls=%async_computation.2 | async-start | bytes 4194304 | tf_op jit(solution)/shard_map/all_to_all | solution.py:54
  160.8 25.4 %all-to-all-done.2 = bf16[16,16,4096]{2,1,0:T(8,128)(2,1)} async-done(((bf16[16,16,4096]{2,1,0:T(8,128)(2,1)}), bf16[16,16,4096]{2,1,0:T(8,128)(2,1)}, u32[]{:S(2)}, u32[]{:S(2)}) %all-to-all-start.2) | async-done | bytes 2097184 | tf_op jit(solution)/shard_map/all_to_all | solution.py:54
  194.8 5.6 %fusion.13 = (bf16[4096,256]{1,0:T(8,128)(2,1)S(1)}, bf16[4096,256]{1,0:T(8,128)(2,1)}) fusion(bf16[1,1024,256]{2,1,0:T(8,128)(2,1)} %collective-permute-done.5, bf16[1,1024,256]{2,1,0:T(8,128)(2,1)} %collective-permute-done.4, bf16[1,1024,256]{2,1,0:T(8,128)(2,1)} %collective-permute-done.3, bf16[1,1024,256]{2,1,0:T(8,128)(2,1)} %convert_bitcast_fusion, ...), kind=kOutput, calls=%fused_computation.39 | convolution fusion | flops 555745280 | bytes 8519680 | tf_op jit(solution)/shard_map/dot_general | solution.py:24
  200.5 22.7 %all-gather.3.cloned.1.call-done = bf16[256,4096]{1,0:T(8,128)(2,1)} async-done(((bf16[16,4096]{1,0:T(8,128)(2,1)}), bf16[256,4096]{1,0:T(8,128)(2,1)}) %all-gather.3.cloned.1.call-update) | async-done | bytes 2097168 | tf_op jit(solution)/shard_map/all_gather | solution.py:118
  223.2 5.1 %fusion.49 = f32[256,256]{1,0:T(8,128)S(1)} fusion(bf16[256,4096]{1,0:T(8,128)(2,1)} %all-gather.3.cloned.1.call-done, f32[4096,256]{1,0:T(8,128)} %convolution_multiply_fusion.3, bf16[2,4096,256]{2,1,0:T(8,128)(2,1)} %pad_maximum_fusion), kind=kOutput, calls=%fused_computation.81 | convolution fusion | flops 545325056 | bytes 8650752 | tf_op jit(solution)/shard_map/dot_general | solution.py:126
  232.7 31.3 %all_to_all.26 = bf16[16,16,4096]{2,1,0:T(8,128)(2,1)S(1)} all-to-all(bf16[16,16,4096]{2,1,0:T(8,128)(2,1)S(1)} %bitcast.124), channel_id=1, replica_groups=mesh['a'=2,'c'=2,'h'=4,'y'=4,'x'=4] {'y','x'}, dimensions={0} | all-to-all | bytes 4194304 | tf_op jit(solution)/shard_map/all_to_all | solution.py:62
  264.3 3.9 %collective-permute-start.11 = (bf16[16,4096]{1,0:T(8,128)(2,1)S(1)}, bf16[16,4096]{1,0:T(8,128)(2,1)S(1)}, u32[]{:S(2)}, u32[]{:S(2)}) collective-permute-start(bf16[16,4096]{1,0:T(8,128)(2,1)S(1)} %convert_element_type.237), channel_id=1, source_target_pairs={{0,48},{16,0},{32,16},{48,32},{1,49},{17,1},{33,17},{49,33},{2,50}... | collective-permute-start | bytes 393224 | tf_op jit(solution)/shard_map/ppermute | solution.py:71
  268.2 10.5 %collective-permute-start.10 = (bf16[16,4096]{1,0:T(8,128)(2,1)S(1)}, bf16[16,4096]{1,0:T(8,128)(2,1)S(1)}, u32[]{:S(2)}, u32[]{:S(2)}) collective-permute-start(bf16[16,4096]{1,0:T(8,128)(2,1)S(1)} %convert_element_type.237), channel_id=1, source_target_pairs={{0,32},{16,48},{32,0},{48,16},{1,33},{17,49},{33,1},{49,17},{2,34}... | collective-permute-start | bytes 393224 | tf_op jit(solution)/shard_map/ppermute | solution.py:71
  280.9 3.8 collective-permute-done.10
  284.7 3.9 %collective-permute-done.9 = bf16[16,4096]{1,0:T(8,128)(2,1)S(1)} collective-permute-done((bf16[16,4096]{1,0:T(8,128)(2,1)S(1)}, bf16[16,4096]{1,0:T(8,128)(2,1)S(1)}, u32[]{:S(2)}, u32[]{:S(2)}) %collective-permute-start.9) | collective-permute-done | bytes 131104 | tf_op jit(solution)/shard_map/ppermute | solution.py:71
  289.0 30.4 %all_to_all.27 = bf16[16,16,4096]{2,1,0:T(8,128)(2,1)S(1)} all-to-all(bf16[16,16,4096]{2,1,0:T(8,128)(2,1)S(1)} %broadcast_in_dim.27), channel_id=1, replica_groups=mesh['a'=2,'c'=2,'h'=4,'y'=4,'x'=4] {'y','x'}, dimensions={0} | all-to-all | bytes 4194304 | tf_op jit(solution)/shard_map/all_to_all | solution.py:54
  320.2 5.0 %fusion.4 = bf16[4096,256]{1,0:T(8,128)(2,1)S(1)} fusion(f32[4096,256]{1,0:T(8,128)S(1)} %copy-done.2, bf16[2,4096,256]{2,1,0:T(8,128)(2,1)S(1)} %copy-done.5, bf16[256,4096]{1,0:T(8,128)(2,1)S(1)} %copy-done.19, f32[256,256]{1,0:T(8,128)S(1)} %copy-done.24, f32[256,256]{1,0:T(8,128)S(1)} %convolution_multiply_fusion.5, f32[256,256]{1,0:T(8,128)S(1)} %copy-done.25), kind=kOutput, calls=%fused_computation.30 | convolution fusion | flops 561643520 | bytes 11272192 | tf_op jit(solution)/shard_map/dot_general | solution.py:24
  325.3 6.2 %fusion.16 = bf16[4096,256]{1,0:T(8,128)(2,1)S(1)} fusion(bf16[4096,256]{1,0:T(8,128)(2,1)S(1)} %copy-done.22, bf16[1,1024,256]{2,1,0:T(8,128)(2,1)} %collective-permute-done.5, bf16[1,1024,256]{2,1,0:T(8,128)(2,1)} %collective-permute-done.4, bf16[1,1024,256]{2,1,0:T(8,128)(2,1)} %collective-permute-done.3, bf16[1,1024,256]{2,1,0:T(8,128)(2,1)} %convert_bitcast_fusion, ...), kind=kOutput, calls=%fused_computation.42 | convolution fusion | flops 568328192 | bytes 8519680 | tf_op jit(solution)/shard_map/dot_general | solution.py:24
  335.1 5.0 %fusion.11 = bf16[4096,256]{1,0:T(8,128)(2,1)S(1)} fusion(f32[4096,256]{1,0:T(8,128)S(1)} %copy-done.1, bf16[2,4096,256]{2,1,0:T(8,128)(2,1)S(1)} %copy-done.5, bf16[256,4096]{1,0:T(8,128)(2,1)S(1)} %copy-done.19, f32[256,256]{1,0:T(8,128)S(1)} %convolution_multiply_fusion.5, f32[256,256]{1,0:T(8,128)S(1)} %copy-done.24), kind=kOutput, calls=%fused_computation.37 | convolution fusion | flops 561381376 | bytes 11010048 | tf_op jit(solution)/shard_map/dot_general | solution.py:24
  342.2 4.9 %collective-permute-start.17 = (bf16[1024,256]{1,0:T(8,128)(2,1)S(1)}, bf16[1024,256]{1,0:T(8,128)(2,1)S(1)}, u32[]{:S(2)}, u32[]{:S(2)}) collective-permute-start(bf16[1024,256]{1,0:T(8,128)(2,1)S(1)} %fusion.55), channel_id=1, source_target_pairs={{0,128},{128,0},{1,129},{129,1},{2,130},{130,2},{3,131},{131,3},{4... | collective-permute-start | bytes 1572872 | tf_op jit(solution)/shard_map/ppermute | solution.py:40
  349.2 10.2 %collective-permute-done.17 = bf16[1024,256]{1,0:T(8,128)(2,1)S(1)} collective-permute-done((bf16[1024,256]{1,0:T(8,128)(2,1)S(1)}, bf16[1024,256]{1,0:T(8,128)(2,1)S(1)}, u32[]{:S(2)}, u32[]{:S(2)}) %collective-permute-start.17) | collective-permute-done | bytes 524320 | tf_op jit(solution)/shard_map/ppermute | solution.py:40
  361.2 9.5 %collective-permute-done.13 = bf16[1024,256]{1,0:T(8,128)(2,1)S(1)} collective-permute-done((bf16[1024,256]{1,0:T(8,128)(2,1)S(1)}, bf16[1024,256]{1,0:T(8,128)(2,1)S(1)}, u32[]{:S(2)}, u32[]{:S(2)}) %collective-permute-start.13) | collective-permute-done | bytes 524320 | tf_op jit(solution)/shard_map/ppermute | solution.py:40
  372.4 9.5 %collective-permute-done.15 = bf16[1024,256]{1,0:T(8,128)(2,1)S(1)} collective-permute-done((bf16[1024,256]{1,0:T(8,128)(2,1)S(1)}, bf16[1024,256]{1,0:T(8,128)(2,1)S(1)}, u32[]{:S(2)}, u32[]{:S(2)}) %collective-permute-start.15) | collective-permute-done | bytes 524320 | tf_op jit(solution)/shard_map/ppermute | solution.py:40
  (135 shorter events, 69.0 us)
Async XLA Ops:
  9.9 59.8 %collective-permute-start.1 = (bf16[2,1024,256]{2,1,0:T(8,128)(2,1)}, bf16[2,1024,256]{2,1,0:T(8,128)(2,1)}, u32[]{:S(2)}, u32[]{:S(2)}) collective-permute-start(bf16[2,1024,256]{2,1,0:T(8,128)(2,1)} %pad_maximum_fusion.1), channel_id=1, source_target_pairs={{0,128},{128,0},{1,129},{129,1},{2,130},{130,2},{3,131},{131,3},{4... | collective-permute-start | bytes 3145736 | tf_op jit(solution)/shard_map/ppermute | solution.py:40
  59.6 36.9 %all-to-all-start = ((bf16[16,16,4096]{2,1,0:T(8,128)(2,1)}), bf16[16,16,4096]{2,1,0:T(8,128)(2,1)S(1)}, u32[]{:S(2)}, u32[]{:S(2)}) async-start(bf16[16,16,4096]{2,1,0:T(8,128)(2,1)} %broadcast_in_dim.11), calls=%async_computation | async-start | bytes 4194304 | tf_op jit(solution)/shard_map/all_to_all | solution.py:54
  66.0 20.6 %collective-permute-start = (bf16[2,1024,256]{2,1,0:T(8,128)(2,1)}, bf16[2,1024,256]{2,1,0:T(8,128)(2,1)S(1)}, u32[]{:S(2)}, u32[]{:S(2)}) collective-permute-start(bf16[2,1024,256]{2,1,0:T(8,128)(2,1)} %pad_maximum_fusion.1), channel_id=1, source_target_pairs={{0,64},{64,0},{1,65},{65,1},{2,66},{66,2},{3,67},{67,3},{4,68},{68... | collective-permute-start | bytes 3145736 | tf_op jit(solution)/shard_map/ppermute | solution.py:36
  69.7 16.8 %collective-permute-start.2 = (bf16[2,1024,256]{2,1,0:T(8,128)(2,1)}, bf16[2,1024,256]{2,1,0:T(8,128)(2,1)S(1)}, u32[]{:S(2)}, u32[]{:S(2)}) collective-permute-start(bf16[2,1024,256]{2,1,0:T(8,128)(2,1)} %collective-permute-done.1), channel_id=1, source_target_pairs={{0,64},{64,0},{1,65},{65,1},{2,66},{66,2},{3,67},{67,3},{4,68},{68... | collective-permute-start | bytes 3145736 | tf_op jit(solution)/shard_map/ppermute | solution.py:36
  71.9 13.4 %collective-permute-start.4 = (bf16[1,1024,256]{2,1,0:T(8,128)(2,1)}, bf16[1,1024,256]{2,1,0:T(8,128)(2,1)}, u32[]{:S(2)}, u32[]{:S(2)}) collective-permute-start(bf16[1,1024,256]{2,1,0:T(8,128)(2,1)} %convert_bitcast_fusion), channel_id=1, source_target_pairs={{0,128},{128,0},{1,129},{129,1},{2,130},{130,2},{3,131},{131,3},{4... | collective-permute-start | bytes 1572872 | tf_op jit(solution)/shard_map/ppermute | solution.py:40
  73.2 27.6 %collective-permute-start.3 = (bf16[1,1024,256]{2,1,0:T(8,128)(2,1)}, bf16[1,1024,256]{2,1,0:T(8,128)(2,1)}, u32[]{:S(2)}, u32[]{:S(2)}) collective-permute-start(bf16[1,1024,256]{2,1,0:T(8,128)(2,1)} %convert_bitcast_fusion), channel_id=1, source_target_pairs={{0,64},{64,0},{1,65},{65,1},{2,66},{66,2},{3,67},{67,3},{4,68},{68... | collective-permute-start | bytes 1572872 | tf_op jit(solution)/shard_map/ppermute | solution.py:36
  85.3 15.5 %collective-permute-start.5 = (bf16[1,1024,256]{2,1,0:T(8,128)(2,1)}, bf16[1,1024,256]{2,1,0:T(8,128)(2,1)}, u32[]{:S(2)}, u32[]{:S(2)}) collective-permute-start(bf16[1,1024,256]{2,1,0:T(8,128)(2,1)} %collective-permute-done.4), channel_id=1, source_target_pairs={{0,64},{64,0},{1,65},{65,1},{2,66},{66,2},{3,67},{67,3},{4,68},{68... | collective-permute-start | bytes 1572872 | tf_op jit(solution)/shard_map/ppermute | solution.py:36
  103.1 41.8 %copy-start.10 = (f32[1,4,4,4096]{3,2,1,0:T(4,128)S(1)}, f32[1,4,4,4096]{3,2,1,0:T(4,128)}, u32[]{:S(2)}) copy-start(f32[1,4,4,4096]{3,2,1,0:T(4,128)} %get-tuple-element.34) | copy-start | bytes 786436
  139.0 6.7 %collective-permute-start.8 = (bf16[16,4096]{1,0:T(8,128)(2,1)}, bf16[16,4096]{1,0:T(8,128)(2,1)}, u32[]{:S(2)}, u32[]{:S(2)}) collective-permute-start(bf16[16,4096]{1,0:T(8,128)(2,1)} %convert_element_type.218), channel_id=1, source_target_pairs={{0,48},{16,0},{32,16},{48,32},{1,49},{17,1},{33,17},{49,33},{2,50}... | collective-permute-start | bytes 393224 | tf_op jit(solution)/shard_map/ppermute | solution.py:71
  140.7 9.9 %collective-permute-start.7 = (bf16[16,4096]{1,0:T(8,128)(2,1)}, bf16[16,4096]{1,0:T(8,128)(2,1)}, u32[]{:S(2)}, u32[]{:S(2)}) collective-permute-start(bf16[16,4096]{1,0:T(8,128)(2,1)} %convert_element_type.218), channel_id=1, source_target_pairs={{0,32},{16,48},{32,0},{48,16},{1,33},{17,49},{33,1},{49,17},{2,34}... | collective-permute-start | bytes 393224 | tf_op jit(solution)/shard_map/ppermute | solution.py:71
  143.3 9.5 %collective-permute-start.6 = (bf16[16,4096]{1,0:T(8,128)(2,1)}, bf16[16,4096]{1,0:T(8,128)(2,1)}, u32[]{:S(2)}, u32[]{:S(2)}) collective-permute-start(bf16[16,4096]{1,0:T(8,128)(2,1)} %convert_element_type.218), channel_id=1, source_target_pairs={{0,16},{16,32},{32,48},{48,0},{1,17},{17,33},{33,49},{49,1},{2,18}... | collective-permute-start | bytes 393224 | tf_op jit(solution)/shard_map/ppermute | solution.py:71
  155.6 30.6 %all-to-all-start.2 = ((bf16[16,16,4096]{2,1,0:T(8,128)(2,1)}), bf16[16,16,4096]{2,1,0:T(8,128)(2,1)}, u32[]{:S(2)}, u32[]{:S(2)}) async-start(bf16[16,16,4096]{2,1,0:T(8,128)(2,1)} %broadcast_in_dim.26), calls=%async_computation.2 | async-start | bytes 4194304 | tf_op jit(solution)/shard_map/all_to_all | solution.py:54
  160.0 63.2 %all-gather.3.cloned.1.call-start = ((), (), s32[]{:S(2)}) async-start(), calls=%async_computation.5 | async-start | bytes 2228224 | tf_op jit(solution)/shard_map/all_gather | solution.py:118
  264.3 16.6 %collective-permute-start.11 = (bf16[16,4096]{1,0:T(8,128)(2,1)S(1)}, bf16[16,4096]{1,0:T(8,128)(2,1)S(1)}, u32[]{:S(2)}, u32[]{:S(2)}) collective-permute-start(bf16[16,4096]{1,0:T(8,128)(2,1)S(1)} %convert_element_type.237), channel_id=1, source_target_pairs={{0,48},{16,0},{32,16},{48,32},{1,49},{17,1},{33,17},{49,33},{2,50}... | collective-permute-start | bytes 393224 | tf_op jit(solution)/shard_map/ppermute | solution.py:71
  268.2 16.5 %collective-permute-start.10 = (bf16[16,4096]{1,0:T(8,128)(2,1)S(1)}, bf16[16,4096]{1,0:T(8,128)(2,1)S(1)}, u32[]{:S(2)}, u32[]{:S(2)}) collective-permute-start(bf16[16,4096]{1,0:T(8,128)(2,1)S(1)} %convert_element_type.237), channel_id=1, source_target_pairs={{0,32},{16,48},{32,0},{48,16},{1,33},{17,49},{33,1},{49,17},{2,34}... | collective-permute-start | bytes 393224 | tf_op jit(solution)/shard_map/ppermute | solution.py:71
  278.7 9.9 %collective-permute-start.9 = (bf16[16,4096]{1,0:T(8,128)(2,1)S(1)}, bf16[16,4096]{1,0:T(8,128)(2,1)S(1)}, u32[]{:S(2)}, u32[]{:S(2)}) collective-permute-start(bf16[16,4096]{1,0:T(8,128)(2,1)S(1)} %convert_element_type.237), channel_id=1, source_target_pairs={{0,16},{16,32},{32,48},{48,0},{1,17},{17,33},{33,49},{49,1},{2,18}... | collective-permute-start | bytes 393224 | tf_op jit(solution)/shard_map/ppermute | solution.py:71
  288.6 31.5 %copy-start.25 = (f32[256,256]{1,0:T(8,128)S(1)}, f32[256,256]{1,0:T(8,128)}, u32[]{:S(2)}) copy-start(f32[256,256]{1,0:T(8,128)} %get-tuple-element.39) | copy-start | bytes 786436
  288.7 31.4 %copy-start.19 = (bf16[256,4096]{1,0:T(8,128)(2,1)S(1)}, bf16[256,4096]{1,0:T(8,128)(2,1)}, u32[]{:S(2)}) copy-start(bf16[256,4096]{1,0:T(8,128)(2,1)} %all-gather.3.cloned.1.call-done) | copy-start | bytes 6291460
  331.7 10.4 %collective-permute-start.16 = (bf16[2,1024,256]{2,1,0:T(8,128)(2,1)S(1)}, bf16[2,1024,256]{2,1,0:T(8,128)(2,1)S(1)}, u32[]{:S(2)}, u32[]{:S(2)}) collective-permute-start(bf16[2,1024,256]{2,1,0:T(8,128)(2,1)S(1)} %pad_maximum_fusion.4), channel_id=1, source_target_pairs={{0,64},{64,0},{1,65},{65,1},{2,66},{66,2},{3,67},{67,3},{4,68},{68... | collective-permute-start | bytes 3145736 | tf_op jit(solution)/shard_map/ppermute | solution.py:36
  335.0 12.2 %collective-permute-start.12 = (bf16[2,1024,256]{2,1,0:T(8,128)(2,1)S(1)}, bf16[2,1024,256]{2,1,0:T(8,128)(2,1)S(1)}, u32[]{:S(2)}, u32[]{:S(2)}) collective-permute-start(bf16[2,1024,256]{2,1,0:T(8,128)(2,1)S(1)} %pad_maximum_fusion.2), channel_id=1, source_target_pairs={{0,64},{64,0},{1,65},{65,1},{2,66},{66,2},{3,67},{67,3},{4,68},{68... | collective-permute-start | bytes 3145736 | tf_op jit(solution)/shard_map/ppermute | solution.py:36
  340.3 7.1 %collective-permute-start.14 = (bf16[2,1024,256]{2,1,0:T(8,128)(2,1)S(1)}, bf16[2,1024,256]{2,1,0:T(8,128)(2,1)S(1)}, u32[]{:S(2)}, u32[]{:S(2)}) collective-permute-start(bf16[2,1024,256]{2,1,0:T(8,128)(2,1)S(1)} %pad_maximum_fusion.3), channel_id=1, source_target_pairs={{0,64},{64,0},{1,65},{65,1},{2,66},{66,2},{3,67},{67,3},{4,68},{68... | collective-permute-start | bytes 3145736 | tf_op jit(solution)/shard_map/ppermute | solution.py:36
  342.2 17.2 %collective-permute-start.17 = (bf16[1024,256]{1,0:T(8,128)(2,1)S(1)}, bf16[1024,256]{1,0:T(8,128)(2,1)S(1)}, u32[]{:S(2)}, u32[]{:S(2)}) collective-permute-start(bf16[1024,256]{1,0:T(8,128)(2,1)S(1)} %fusion.55), channel_id=1, source_target_pairs={{0,128},{128,0},{1,129},{129,1},{2,130},{130,2},{3,131},{131,3},{4... | collective-permute-start | bytes 1572872 | tf_op jit(solution)/shard_map/ppermute | solution.py:40
  347.3 23.4 %collective-permute-start.13 = (bf16[1024,256]{1,0:T(8,128)(2,1)S(1)}, bf16[1024,256]{1,0:T(8,128)(2,1)S(1)}, u32[]{:S(2)}, u32[]{:S(2)}) collective-permute-start(bf16[1024,256]{1,0:T(8,128)(2,1)S(1)} %fusion.61), channel_id=1, source_target_pairs={{0,128},{128,0},{1,129},{129,1},{2,130},{130,2},{3,131},{131,3},{4... | collective-permute-start | bytes 1572872 | tf_op jit(solution)/shard_map/ppermute | solution.py:40
  347.6 34.3 %collective-permute-start.15 = (bf16[1024,256]{1,0:T(8,128)(2,1)S(1)}, bf16[1024,256]{1,0:T(8,128)(2,1)S(1)}, u32[]{:S(2)}, u32[]{:S(2)}) collective-permute-start(bf16[1024,256]{1,0:T(8,128)(2,1)S(1)} %fusion.58), channel_id=1, source_target_pairs={{0,128},{128,0},{1,129},{129,1},{2,130},{130,2},{3,131},{131,3},{4... | collective-permute-start | bytes 1572872 | tf_op jit(solution)/shard_map/ppermute | solution.py:40
  (23 other events, 286.7 us)
Sparse Core Ops, SparseCore 0:
  163.9 59.3 all-gather.2

commit v2 on v1

v2 whole, which is shorter than its diff:
```python
import math

import jax
import jax.numpy as jnp
from jax import lax
from jax.sharding import Mesh, PartitionSpec as P

ITERS = 2
BETA_ONE = 0.9
BETA_TWO = 0.95
INNER_RATE = 0.05
DECAY_RATE = 0.1
OUTER_RATE = 0.7
MOMENTUM_RATE = 0.9

AXES = ("a", "c", "h", "y", "u", "v")
SIZES = (2, 2, 4, 4, 2, 2)
HEIGHT = 4
PLANE = ("y", "u")
BF16 = jnp.bfloat16
F32 = jnp.float32
SWAP = ((0, 1), (1, 0))
HEIGHT_PAIRS = (((0, 1), (1, 0), (2, 3), (3, 2)), ((0, 3), (3, 0), (1, 2), (2, 1)))


def contract_rows(left, right):
    return lax.dot_general(
        left, right, (((0,), (0,)), ((), ())), preferred_element_type=F32
    )


def contract_cols(left, right):
    return lax.dot_general(
        left, right, (((1,), (1,)), ((), ())), preferred_element_type=F32
    )


def after(value, *others):
    return lax.optimization_barrier((value,) + others)[0]


def own_first(value):
    count, width = value.shape
    parts = value.reshape(count, 2, 2, width // 4)
    parts = jnp.where(lax.axis_index("c") == 1, parts[:, :, ::-1], parts)
    return parts.reshape(count, 2, width // 2)


def regroup(value):
    column = lax.axis_index("v")
    pieces = []
    for flip, pairs in (
        (0, ((0, 0), (1, 2), (2, 1), (3, 3))),
        (1, ((0, 2), (1, 0), (2, 3), (3, 1))),
    ):
        part = lax.dynamic_index_in_dim(value, column ^ flip, 1, keepdims=False)
        pieces.append(lax.ppermute(part, ("a", "v"), pairs))
    low = lax.axis_index("a") == 0
    return jnp.stack(
        [
            jnp.where(low, pieces[0], pieces[1]),
            jnp.where(low, pieces[1], pieces[0]),
        ]
    )


def gather_height(value):
    place = lax.axis_index("h")
    value = value[None]
    for pairs, low in zip(HEIGHT_PAIRS, (place % 2 == 0, place < 2)):
        other = lax.ppermute(value, "h", pairs)
        value = jnp.concatenate(
            [jnp.where(low, value, other), jnp.where(low, other, value)], axis=0
        )
    return value


def spread_plane(value):
    copies = lax.psum(1, PLANE)
    return lax.all_to_all(
        jnp.broadcast_to(value[None], (copies,) + value.shape), PLANE, 0, 0
    ).reshape((copies * value.shape[0],) + value.shape[1:])


def sum_plane(value):
    copies = lax.psum(1, PLANE)
    parts = value.reshape((copies, value.shape[0] // copies) + value.shape[1:])
    parts = lax.all_to_all(parts, PLANE, 0, 0)
    return jnp.sum(parts.astype(F32), axis=0)


def sum_height(value):
    for pairs in HEIGHT_PAIRS:
        value = value + lax.ppermute(value.astype(BF16), "h", pairs).astype(F32)
    return value


def other_half(value):
    return lax.ppermute(value.astype(BF16), "a", SWAP)


def per_device(
    outer_gate,
    outer_up,
    outer_down,
    momentum_gate,
    momentum_up,
    momentum_down,
    inputs,
    targets,
    loss_flags,
):
    tokens = inputs.shape[2]
    features = inputs.shape[3]
    rows, width = outer_gate.shape
    half = features // 2
    group = 2 * HEIGHT * tokens
    total_rows = tokens * 64
    hidden_units = width * 64
    scale_in = features ** (-0.5)
    scale_hidden = hidden_units ** (-0.5)
    epsilon = 1.0 / math.sqrt(hidden_units * total_rows)

    flag_rows = jnp.zeros((ITERS, 2, half), BF16)
    flag_rows = flag_rows.at[:, :, :tokens].set(
        loss_flags[:, 0].astype(BF16)[:, None, :]
    )
    packed = jnp.concatenate(
        [
            own_first(
                jnp.concatenate(
                    [inputs[0, 0], inputs[1, 0], targets[0, 0], targets[1, 0]], axis=0
                )
            ),
            flag_rows,
        ],
        axis=0,
    )
    packed = regroup(packed)

    own = jnp.stack([outer_gate, outer_up, outer_down]).astype(BF16)
    own, packed = lax.optimization_barrier((own, packed))
    side = lax.ppermute(own, "v", SWAP)
    near = lax.ppermute(own, "c", SWAP)

    column = gather_height(packed)
    x_rows = [
        column[:, :, s * tokens : (1 + s) * tokens].reshape(group, half)
        for s in range(ITERS)
    ]
    t_rows = [
        column[:, :, (2 + s) * tokens : (3 + s) * tokens].reshape(group, half)
        for s in range(ITERS)
    ]
    flags = [
        column[:, :, 4 * tokens + s, :tokens].reshape(group, 1).astype(F32)
        for s in range(ITERS)
    ]
    x_first, side = lax.optimization_barrier((x_rows[0], side))
    batch_one = spread_plane(x_first)
    near_side = lax.ppermute(side, "c", SWAP)
    start = [
        [
            jnp.concatenate([own[index], near[index]], axis=0),
            jnp.concatenate([side[index], near_side[index]], axis=0),
        ]
        for index in range(3)
    ]

    keep = 1.0 - INNER_RATE * DECAY_RATE
    m_one = BETA_ONE * (1.0 - BETA_ONE) / (1.0 - BETA_ONE**2)
    m_two = (1.0 - BETA_ONE) / (1.0 - BETA_ONE**2)
    v_one = BETA_TWO * (1.0 - BETA_TWO) / (1.0 - BETA_TWO**2)
    v_two = (1.0 - BETA_TWO) / (1.0 - BETA_TWO**2)

    def first_update(w, g):
        return (
            keep * w.astype(F32) - INNER_RATE * (g / (jnp.abs(g) + epsilon))
        ).astype(BF16)

    def both_updates(w, p, g):
        p = p.astype(F32)
        u_one = p / (jnp.abs(p) + epsilon)
        u_two = (m_one * p + m_two * g) / (
            jnp.sqrt(v_one * p * p + v_two * g * g) + epsilon
        )
        return (
            (1.0 - keep * keep) * w.astype(F32)
            + (keep * INNER_RATE) * u_one
            + INNER_RATE * u_two
        ).astype(BF16)

    def partial_pre(batch, w_gate, w_up):
        return jnp.stack(
            [
                jnp.dot(batch, w_gate, preferred_element_type=F32),
                jnp.dot(batch, w_up, preferred_element_type=F32),
            ]
        )

    def gated(pre):
        return (pre[0] * jax.nn.sigmoid(pre[0]) * pre[1]).astype(BF16)

    def output_sum(hidden, w_down):
        partial = contract_cols(hidden[0], w_down[0]) + contract_cols(
            hidden[1], w_down[1]
        )
        return sum_plane((partial * scale_hidden).astype(BF16))

    def hidden_partial(out_grad, w_down):
        return jnp.stack(
            [jnp.dot(out_grad, w, preferred_element_type=F32) for w in w_down]
        )

    def hidden_grads(hidden_grad, pre):
        hidden_grad = hidden_grad * scale_hidden
        pairs = []
        for side in range(2):
            gate_pre, up_pre = pre[side][0], pre[side][1]
            sigma = jax.nn.sigmoid(gate_pre)
            gate_grad = (
                hidden_grad[side] * up_pre * sigma * (1.0 + gate_pre * (1.0 - sigma))
            ).astype(BF16)
            up_grad = (hidden_grad[side] * (gate_pre * sigma)).astype(BF16)
            pairs.append((gate_grad, up_grad))
        return pairs

    sides = range(2)
    partial = [partial_pre(batch_one, start[0][k], start[1][k]) for k in sides]
    def own_grad(step, total):
        return (
            flags[step] * (total - t_rows[step].astype(F32)) / total_rows
        ).astype(BF16)

    others = [other_half(item) for item in partial]
    batch_two = spread_plane(after(x_rows[1], *partial))
    others = after(others, batch_two)
    pre = [(partial[k] + others[k].astype(F32)) * scale_in for k in sides]
    hidden = [gated(item) for item in pre]
    out_grad = spread_plane(own_grad(0, sum_height(output_sum(hidden, start[2]))))
    partial = hidden_partial(out_grad, start[2])
    pairs = hidden_grads(partial + other_half(partial).astype(F32), pre)
    grads = [
        [contract_rows(batch_one, pairs[k][0]) * scale_in for k in sides],
        [contract_rows(batch_one, pairs[k][1]) * scale_in for k in sides],
        [
            contract_rows(after(out_grad, partial), hidden[k]) * scale_hidden
            for k in sides
        ],
    ]
    weights = [[first_update(start[i][k], grads[i][k]) for k in sides] for i in range(3)]
    first = [[grads[i][k].astype(BF16) for k in sides] for i in range(3)]

    partial = [partial_pre(batch_two, weights[0][k], weights[1][k]) for k in sides]
    pre = [(item + other_half(item).astype(F32)) * scale_in for item in partial]
    hidden = [gated(item) for item in pre]
    out_grad = spread_plane(own_grad(1, sum_height(output_sum(hidden, weights[2]))))
    partial = hidden_partial(out_grad, weights[2])
    other = other_half(partial)
    out_grad = after(out_grad, partial)

    def update(index, side, left, right, scale):
        return both_updates(
            start[index][side], first[index][side], contract_rows(left, right) * scale
        )

    def own_rows(delta):
        near = lax.ppermute(delta[rows:], "c", SWAP)
        return delta[:rows].astype(F32) + near.astype(F32)

    partner = [None] * 3
    delta = update(2, 1, out_grad, hidden[1], scale_hidden)
    sent = own_rows(delta).astype(BF16)
    partner[2] = lax.ppermute(sent, "v", SWAP)
    pairs = hidden_grads(partial + after(other, partner[2]).astype(F32), pre)
    delta = update(0, 1, batch_two, pairs[1][0], scale_in)
    sent_gate = own_rows(delta).astype(BF16)
    partner[0] = lax.ppermute(sent_gate, "v", SWAP)
    delta = update(1, 1, after(batch_two, delta), pairs[1][1], scale_in)
    sent = own_rows(delta).astype(BF16)
    partner[1] = lax.ppermute(sent, "v", SWAP)
    batch_two, out_grad = after((batch_two, out_grad), sent_gate, sent)
    left = {0: batch_two, 1: batch_two, 2: out_grad}
    right = {0: pairs[0][0], 1: pairs[0][1], 2: hidden[0]}
    scales = {0: scale_in, 1: scale_in, 2: scale_hidden}
    outer_own = (outer_gate, outer_up, outer_down)
    momenta = (momentum_gate, momentum_up, momentum_down)
    new_params = [None] * 3
    new_momenta = [None] * 3
    for index in (2, 0, 1):
        delta = update(index, 0, left[index], right[index], scales[index])
        total = own_rows(delta) + partner[index].astype(F32)
        average = total / 4.0
        fresh = MOMENTUM_RATE * momenta[index] + average
        new_momenta[index] = fresh
        new_params[index] = outer_own[index] - OUTER_RATE * (
            average + MOMENTUM_RATE * fresh
        )
    return tuple(new_params) + tuple(new_momenta)


def solution(mesh):
    fine = Mesh(mesh.devices.reshape(SIZES), AXES)
    rep, fsdp = AXES[:2], AXES[2:]
    state = P(rep, fsdp)
    rows = P(None, rep, fsdp, None)
    return jax.shard_map(
        per_device,
        mesh=fine,
        in_specs=(state,) * 6 + (rows, rows, P(None, rep, fsdp)),
        out_specs=(state,) * 6,
        check_vma=False,
    )
```

time: 396 us -> 310 us (0.78)
  blocking collectives: 138 us -> 63.2 us
  local copies, waits for them, and re-layouts: 8.99 us -> 22.4 us
  between operations: 14.8 us -> 2.2 us
  starting transfers between devices: 53.6 us -> 64.6 us
  waiting for transfers between devices: 104 us -> 94 us
  other arithmetic: 25.2 us -> 18.5 us
  matrix products: 45.3 us -> 40 us
    all_gather x1 -> x0, blocking collectives: 41.9 us -> none  [per_device(): column = lax.all_gather(packed, 'h', axis=0)]
    all_to_all x2, blocking collectives: 66.2 us -> 34.1 us  [sum_plane(): parts = lax.all_to_all(parts, PLANE, 0, 0)]
    all_gather x1 -> x0, waiting for transfers between devices: 22.7 us -> none  [per_device(): batch_two = lax.all_gather(x_rows[1], PLANE, axis=0, tiled=True)]
    ppermute x18 -> x26, waiting for transfers between devices: 56.2 us -> 76.7 us  [the longest x4 20.1 us: sum_height(): value = value + lax.ppermute(value.astype(BF16), 'h', pairs).astype(F32)]
    ppermute x18 -> x26, starting transfers between devices: 42.8 us -> 53.7 us  [the longest x6 17.1 us: own_rows(): near = lax.ppermute(delta[rows:], 'c', SWAP)]
    concatenate x2, other arithmetic: 10.1 us -> 0.06 us  [the longest x1 0.05 us: gather_height(): jnp.concatenate([jnp.where(low, value, other), jnp.where(low, other, valu...]
    all_to_all x2, waiting for transfers between devices: 25.4 us -> 17.2 us  [spread_plane(): lax.all_to_all(jnp.broadcast_to(value[None], (copies,) + value.shape), PL...]
    squeeze x1 -> x5, local copies, waits for them, and re-layouts: 0.69 us -> 8.34 us  [the longest x1 2.53 us: per_device(): side[index]]
  transfers between devices with their start and end apart: 21 -> 28, of which waited for: 11 -> 17; matrix products, arithmetic and copies ran while one was open for 12% -> 14% of each run, Pallas kernels for 0% -> 0%
where the time goes in v2:
time: 310 us; the launch traced here: 305 us
  waiting for transfers between devices  94 us (30%)
  starting transfers between devices  64.6 us (21%)
  blocking collectives  63.2 us (20%)
  matrix products  40 us (13%)
  local copies, waits for them, and re-layouts  22.4 us (7%)
  other arithmetic  18.5 us (6%)
    all_to_all x2, blocking collectives, sum_plane(): parts = lax.all_to_all(parts, PLANE, 0, 0)  34.1 us
    all_to_all x2, blocking collectives, spread_plane(): lax.all_to_all(jnp.broadcast_to(value[None], (copies,) + value.shape), PL...  29.2 us
    dot_general x12, matrix products, contract_rows(): lax.dot_general(left, right, (((0,), (0,)), ((), ())), preferred_element_...  25.5 us
    ppermute x4, waiting for transfers between devices, sum_height(): value = value + lax.ppermute(value.astype(BF16), 'h', pairs).astype(F32)  20.1 us
    all_to_all x2, waiting for transfers between devices, spread_plane(): lax.all_to_all(jnp.broadcast_to(value[None], (copies,) + value.shape), PL...  17.2 us
    ppermute x6, starting transfers between devices, own_rows(): near = lax.ppermute(delta[rows:], 'c', SWAP)  17.1 us
    ppermute x4, starting transfers between devices, sum_height(): value = value + lax.ppermute(value.astype(BF16), 'h', pairs).astype(F32)  14.7 us
    ppermute x2, waiting for transfers between devices, gather_height(): other = lax.ppermute(value, 'h', pairs)  14.4 us
  transfers between devices with their start and end apart: 28, of which 17 were waited for; matrix products, arithmetic and copies ran while one was open for 14% of the time, Pallas kernels for 0%

profile of v2, /device:TPU:1, one launch (start us, length us, event | category | flops | bytes accessed | tf_op | source)
XLA Modules:
  0.0 304.9 jit_solution(10087086158687120673)
XLA Ops:
  18.9 6.7 %collective-permute-done.3 = bf16[1,2,18,2048]{3,2,1,0:T(8,128)(2,1)S(1)} collective-permute-done((bf16[1,2,18,2048]{3,2,1,0:T(8,128)(2,1)S(1)}, bf16[1,2,18,2048]{3,2,1,0:T(8,128)(2,1)S(1)}, u32[]{:S(2)}, u32[]{:S(2)}) %collective-permute-start.3) | collective-permute-done | bytes 147488 | tf_op jit(solution)/shard_map/ppermute | solution.py:71
  25.8 4.4 %collective-permute-start.2 = (bf16[3,1024,256]{2,1,0:T(8,128)(2,1)S(1)}, bf16[3,1024,256]{2,1,0:T(8,128)(2,1)}, u32[]{:S(2)}, u32[]{:S(2)}) collective-permute-start(bf16[3,1024,256]{2,1,0:T(8,128)(2,1)S(1)} %pad_maximum_fusion), channel_id=1, source_target_pairs={{0,64},{64,0},{1,65},{65,1},{2,66},{66,2},{3,67},{67,3},{4,68},{68... | collective-permute-start | bytes 4718600 | tf_op jit(solution)/shard_map/ppermute | solution.py:144
  30.2 7.7 %collective-permute-done.4 = bf16[2,2,18,2048]{3,2,1,0:T(8,128)(2,1)} collective-permute-done((bf16[2,2,18,2048]{3,2,1,0:T(8,128)(2,1)S(1)}, bf16[2,2,18,2048]{3,2,1,0:T(8,128)(2,1)}, u32[]{:S(2)}, u32[]{:S(2)}) %collective-permute-start.4) | collective-permute-done | bytes 294944 | tf_op jit(solution)/shard_map/ppermute | solution.py:71
  40.0 11.6 %collective-permute-done.5 = bf16[3,1024,256]{2,1,0:T(8,128)(2,1)} collective-permute-done((bf16[3,1024,256]{2,1,0:T(8,128)(2,1)S(1)}, bf16[3,1024,256]{2,1,0:T(8,128)(2,1)}, u32[]{:S(2)}, u32[]{:S(2)}) %collective-permute-start.5) | collective-permute-done | bytes 1572896 | tf_op jit(solution)/shard_map/ppermute | solution.py:143
  55.4 6.7 %all-to-all-start = ((bf16[8,32,2048]{2,1,0:T(8,128)(2,1)}), bf16[8,32,2048]{2,1,0:T(8,128)(2,1)S(1)}, u32[]{:S(2)}, u32[]{:S(2)}) async-start(bf16[8,32,2048]{2,1,0:T(8,128)(2,1)} %broadcast_in_dim.14), calls=%async_computation | async-start | bytes 2097152 | tf_op jit(solution)/shard_map/all_to_all | solution.py:80
  69.0 10.1 %all-to-all-done = bf16[8,32,2048]{2,1,0:T(8,128)(2,1)S(1)} async-done(((bf16[8,32,2048]{2,1,0:T(8,128)(2,1)}), bf16[8,32,2048]{2,1,0:T(8,128)(2,1)S(1)}, u32[]{:S(2)}, u32[]{:S(2)}) %all-to-all-start) | async-done | bytes 1048608 | tf_op jit(solution)/shard_map/all_to_all | solution.py:80
  80.2 4.2 %all-to-all-start.1 = ((bf16[8,32,2048]{2,1,0:T(8,128)(2,1)}), bf16[8,32,2048]{2,1,0:T(8,128)(2,1)}, u32[]{:S(2)}, u32[]{:S(2)}) async-start(bf16[8,32,2048]{2,1,0:T(8,128)(2,1)} %broadcast_in_dim.15), calls=%async_computation.1 | async-start | bytes 2097152 | tf_op jit(solution)/shard_map/all_to_all | solution.py:80
  93.2 7.1 %all-to-all-done.1 = bf16[8,32,2048]{2,1,0:T(8,128)(2,1)} async-done(((bf16[8,32,2048]{2,1,0:T(8,128)(2,1)}), bf16[8,32,2048]{2,1,0:T(8,128)(2,1)}, u32[]{:S(2)}, u32[]{:S(2)}) %all-to-all-start.1) | async-done | bytes 1048608 | tf_op jit(solution)/shard_map/all_to_all | solution.py:80
  104.6 19.6 %all_to_all.30 = bf16[8,32,2048]{2,1,0:T(8,128)(2,1)S(1)} all-to-all(bf16[8,32,2048]{2,1,0:T(8,128)(2,1)S(1)} %bitcast.235), channel_id=1, replica_groups=mesh['a'=2,'c'=2,'h'=4,'y'=4,'u'=2,'v'=2] {'y','u'}, dimensions={0} | all-to-all | bytes 2097152 | tf_op jit(solution)/shard_map/all_to_all | solution.py:88
  124.7 6.0 %collective-permute-done.9 = bf16[32,2048]{1,0:T(8,128)(2,1)S(1)} collective-permute-done((bf16[32,2048]{1,0:T(8,128)(2,1)S(1)}, bf16[32,2048]{1,0:T(8,128)(2,1)S(1)}, u32[]{:S(2)}, u32[]{:S(2)}) %collective-permute-start.9) | collective-permute-done | bytes 131104 | tf_op jit(solution)/shard_map/ppermute | solution.py:94
  134.1 4.9 %collective-permute-done.10 = bf16[32,2048]{1,0:T(8,128)(2,1)} collective-permute-done((bf16[32,2048]{1,0:T(8,128)(2,1)}, bf16[32,2048]{1,0:T(8,128)(2,1)}, u32[]{:S(2)}, u32[]{:S(2)}) %collective-permute-start.10) | collective-permute-done | bytes 131104 | tf_op jit(solution)/shard_map/ppermute | solution.py:94
  140.2 14.9 %all_to_all.31 = bf16[8,32,2048]{2,1,0:T(8,128)(2,1)S(1)} all-to-all(bf16[8,32,2048]{2,1,0:T(8,128)(2,1)S(1)} %broadcast_in_dim.16), channel_id=1, replica_groups=mesh['a'=2,'c'=2,'h'=4,'y'=4,'u'=2,'v'=2] {'y','u'}, dimensions={0} | all-to-all | bytes 2097152 | tf_op jit(solution)/shard_map/all_to_all | solution.py:80
  177.6 4.5 %collective-permute-done.13 = bf16[2,256,256]{2,1,0:T(8,128)(2,1)S(1)} collective-permute-done((bf16[2,256,256]{2,1,0:T(8,128)(2,1)S(1)}, bf16[2,256,256]{2,1,0:T(8,128)(2,1)S(1)}, u32[]{:S(2)}, u32[]{:S(2)}) %collective-permute-start.13) | collective-permute-done | bytes 262176 | tf_op jit(solution)/shard_map/ppermute | solution.py:99
  183.9 14.4 %all_to_all.32 = bf16[8,32,2048]{2,1,0:T(8,128)(2,1)S(1)} all-to-all(bf16[8,32,2048]{2,1,0:T(8,128)(2,1)S(1)} %bitcast.236), channel_id=1, replica_groups=mesh['a'=2,'c'=2,'h'=4,'y'=4,'u'=2,'v'=2] {'y','u'}, dimensions={0} | all-to-all | bytes 2097152 | tf_op jit(solution)/shard_map/all_to_all | solution.py:88
  199.8 5.2 %collective-permute-done.14 = bf16[32,2048]{1,0:T(8,128)(2,1)S(1)} collective-permute-done((bf16[32,2048]{1,0:T(8,128)(2,1)S(1)}, bf16[32,2048]{1,0:T(8,128)(2,1)S(1)}, u32[]{:S(2)}, u32[]{:S(2)}) %collective-permute-start.14) | collective-permute-done | bytes 131104 | tf_op jit(solution)/shard_map/ppermute | solution.py:94
  205.7 10.6 %collective-permute-start.15 = (bf16[32,2048]{1,0:T(8,128)(2,1)}, bf16[32,2048]{1,0:T(8,128)(2,1)}, u32[]{:S(2)}, u32[]{:S(2)}) collective-permute-start(bf16[32,2048]{1,0:T(8,128)(2,1)} %fusion.105), channel_id=1, source_target_pairs={{0,48},{48,0},{16,32},{32,16},{1,49},{49,1},{17,33},{33,17},{2,50}... | collective-permute-start | bytes 393224 | tf_op jit(solution)/shard_map/ppermute | solution.py:94
  216.6 4.0 %collective-permute-done.15 = bf16[32,2048]{1,0:T(8,128)(2,1)} collective-permute-done((bf16[32,2048]{1,0:T(8,128)(2,1)}, bf16[32,2048]{1,0:T(8,128)(2,1)}, u32[]{:S(2)}, u32[]{:S(2)}) %collective-permute-start.15) | collective-permute-done | bytes 131104 | tf_op jit(solution)/shard_map/ppermute | solution.py:94
  221.8 14.3 %all_to_all.33 = bf16[8,32,2048]{2,1,0:T(8,128)(2,1)S(1)} all-to-all(bf16[8,32,2048]{2,1,0:T(8,128)(2,1)S(1)} %broadcast_in_dim.17), channel_id=1, replica_groups=mesh['a'=2,'c'=2,'h'=4,'y'=4,'u'=2,'v'=2] {'y','u'}, dimensions={0} | all-to-all | bytes 2097152 | tf_op jit(solution)/shard_map/all_to_all | solution.py:80
  238.5 14.0 %collective-permute-start.17 = (bf16[1024,256]{1,0:T(8,128)(2,1)S(1)}, bf16[1024,256]{1,0:T(8,128)(2,1)S(1)}, u32[]{:S(2)}, u32[]{:S(2)}) collective-permute-start(bf16[1024,256]{1,0:T(8,128)(2,1)S(1)} %slice.248), channel_id=1, source_target_pairs={{0,64},{64,0},{1,65},{65,1},{2,66},{66,2},{3,67},{67,3},{4,68},{68... | collective-permute-start | bytes 1572872 | tf_op jit(solution)/shard_map/ppermute | solution.py:268
  254.9 7.5 %collective-permute-done.16 = bf16[2,256,256]{2,1,0:T(8,128)(2,1)S(1)} collective-permute-done((bf16[2,256,256]{2,1,0:T(8,128)(2,1)S(1)}, bf16[2,256,256]{2,1,0:T(8,128)(2,1)S(1)}, u32[]{:S(2)}, u32[]{:S(2)}) %collective-permute-start.16) | collective-permute-done | bytes 262176 | tf_op jit(solution)/shard_map/ppermute | solution.py:99
  262.4 5.0 %collective-permute-done.18 = bf16[1024,256]{1,0:T(8,128)(2,1)S(1)} collective-permute-done((bf16[1024,256]{1,0:T(8,128)(2,1)S(1)}, bf16[1024,256]{1,0:T(8,128)(2,1)S(1)}, u32[]{:S(2)}, u32[]{:S(2)}) %collective-permute-start.18) | collective-permute-done | bytes 524320 | tf_op jit(solution)/shard_map/ppermute | solution.py:274
  267.6 3.8 %fusion.23 = bf16[2048,256]{1,0:T(8,128)(2,1)S(1)} fusion(f32[2048,256]{1,0:T(8,128)S(1)} %copy-done.69, bf16[1024,256]{1,0:T(8,128)(2,1)S(1)} %copy-done.65, bf16[1024,256]{1,0:T(8,128)(2,1)S(1)} %copy-done.59, bf16[256,2048]{1,0:T(8,128)(2,1)} %bitcast.21, f32[2,256,256]{2,1,0:T(8,128)S(1)} %add_multiply_fusion.3, f32[2,256,256]{2,1,0:T(8,128)S(1)} %copy-done.15), kind=kOutput, calls=%fused_computation.73 | convolution fusion | flops 282722304 | bytes 6029312 | tf_op jit(solution)/shard_map/dot_general | solution.py:27
  278.5 3.8 %fusion.6 = bf16[2048,256]{1,0:T(8,128)(2,1)S(1)} fusion(f32[2048,256]{1,0:T(8,128)S(1)} %copy-done.67, bf16[1024,256]{1,0:T(8,128)(2,1)S(1)} %copy-done.53, bf16[1024,256]{1,0:T(8,128)(2,1)S(1)} %copy-done.50, bf16[256,2048]{1,0:T(8,128)(2,1)} %bitcast.21, f32[2,256,256]{2,1,0:T(8,128)S(1)} %add_multiply_fusion.5, f32[2,256,256]{2,1,0:T(8,128)S(1)} %add_multiply_fusion.3), kind=kOutput, calls=%fused_computation.56 | convolution fusion | flops 282722304 | bytes 6029312 | tf_op jit(solution)/shard_map/dot_general | solution.py:27
  294.3 8.6 %collective-permute-done.24 = bf16[1024,256]{1,0:T(8,128)(2,1)S(1)} collective-permute-done((bf16[1024,256]{1,0:T(8,128)(2,1)S(1)}, bf16[1024,256]{1,0:T(8,128)(2,1)S(1)}, u32[]{:S(2)}, u32[]{:S(2)}) %collective-permute-start.24) | collective-permute-done | bytes 524320 | tf_op jit(solution)/shard_map/ppermute | solution.py:281
  (287 shorter events, 103.2 us)
Async XLA Ops:
  5.3 5.6 %collective-permute-start = (bf16[18,2048]{1,0:T(8,128)(2,1)}, bf16[18,2048]{1,0:T(8,128)(2,1)}, u32[]{:S(2)}, u32[]{:S(2)}) collective-permute-start(bf16[18,2048]{1,0:T(8,128)(2,1)} %get-tuple-element.74), channel_id=1, source_target_pairs={{0,0},{1,128},{128,1},{129,129},{2,2},{3,130},{130,3},{131,131},{4... | collective-permute-start | bytes 221192 | tf_op jit(solution)/shard_map/ppermute | solution.py:57
  7.5 5.6 %collective-permute-start.1 = (bf16[18,2048]{1,0:T(8,128)(2,1)S(1)}, bf16[18,2048]{1,0:T(8,128)(2,1)}, u32[]{:S(2)}, u32[]{:S(2)}) collective-permute-start(bf16[18,2048]{1,0:T(8,128)(2,1)S(1)} %get-tuple-element.75), channel_id=1, source_target_pairs={{0,128},{1,0},{128,129},{129,1},{2,130},{3,2},{130,131},{131,3},{4... | collective-permute-start | bytes 221192 | tf_op jit(solution)/shard_map/ppermute | solution.py:57
  14.1 11.6 %collective-permute-start.3 = (bf16[1,2,18,2048]{3,2,1,0:T(8,128)(2,1)S(1)}, bf16[1,2,18,2048]{3,2,1,0:T(8,128)(2,1)S(1)}, u32[]{:S(2)}, u32[]{:S(2)}) collective-permute-start(bf16[1,2,18,2048]{3,2,1,0:T(8,128)(2,1)S(1)} %bitcast.241), channel_id=1, source_target_pairs={{0,16},{16,0},{32,48},{48,32},{1,17},{17,1},{33,49},{49,33},{2,18}... | collective-permute-start | bytes 442376 | tf_op jit(solution)/shard_map/ppermute | solution.py:71
  17.2 34.5 %collective-permute-start.5 = (bf16[3,1024,256]{2,1,0:T(8,128)(2,1)S(1)}, bf16[3,1024,256]{2,1,0:T(8,128)(2,1)}, u32[]{:S(2)}, u32[]{:S(2)}) collective-permute-start(bf16[3,1024,256]{2,1,0:T(8,128)(2,1)S(1)} %pad_maximum_fusion), channel_id=1, source_target_pairs={{0,1},{1,0},{2,3},{3,2},{4,5},{5,4},{6,7},{7,6},{8,9},{9,8},{10,11... | collective-permute-start | bytes 4718600 | tf_op jit(solution)/shard_map/ppermute | solution.py:143
  25.7 12.2 %collective-permute-start.4 = (bf16[2,2,18,2048]{3,2,1,0:T(8,128)(2,1)S(1)}, bf16[2,2,18,2048]{3,2,1,0:T(8,128)(2,1)}, u32[]{:S(2)}, u32[]{:S(2)}) collective-permute-start(bf16[2,2,18,2048]{3,2,1,0:T(8,128)(2,1)S(1)} %pad_maximum_fusion.13), channel_id=1, source_target_pairs={{0,48},{48,0},{16,32},{32,16},{1,49},{49,1},{17,33},{33,17},{2,50}... | collective-permute-start | bytes 884744 | tf_op jit(solution)/shard_map/ppermute | solution.py:71
  25.8 40.7 %collective-permute-start.2 = (bf16[3,1024,256]{2,1,0:T(8,128)(2,1)S(1)}, bf16[3,1024,256]{2,1,0:T(8,128)(2,1)}, u32[]{:S(2)}, u32[]{:S(2)}) collective-permute-start(bf16[3,1024,256]{2,1,0:T(8,128)(2,1)S(1)} %pad_maximum_fusion), channel_id=1, source_target_pairs={{0,64},{64,0},{1,65},{65,1},{2,66},{66,2},{3,67},{67,3},{4,68},{68... | collective-permute-start | bytes 4718600 | tf_op jit(solution)/shard_map/ppermute | solution.py:144
  51.6 36.3 %collective-permute-start.7 = (bf16[3,1024,256]{2,1,0:T(8,128)(2,1)}, bf16[3,1024,256]{2,1,0:T(8,128)(2,1)}, u32[]{:S(2)}, u32[]{:S(2)}) collective-permute-start(bf16[3,1024,256]{2,1,0:T(8,128)(2,1)} %collective-permute-done.5), channel_id=1, source_target_pairs={{0,64},{64,0},{1,65},{65,1},{2,66},{66,2},{3,67},{67,3},{4,68},{68... | collective-permute-start | bytes 4718600 | tf_op jit(solution)/shard_map/ppermute | solution.py:161
  55.4 23.7 %all-to-all-start = ((bf16[8,32,2048]{2,1,0:T(8,128)(2,1)}), bf16[8,32,2048]{2,1,0:T(8,128)(2,1)S(1)}, u32[]{:S(2)}, u32[]{:S(2)}) async-start(bf16[8,32,2048]{2,1,0:T(8,128)(2,1)} %broadcast_in_dim.14), calls=%async_computation | async-start | bytes 2097152 | tf_op jit(solution)/shard_map/all_to_all | solution.py:80
  80.2 20.1 %all-to-all-start.1 = ((bf16[8,32,2048]{2,1,0:T(8,128)(2,1)}), bf16[8,32,2048]{2,1,0:T(8,128)(2,1)}, u32[]{:S(2)}, u32[]{:S(2)}) async-start(bf16[8,32,2048]{2,1,0:T(8,128)(2,1)} %broadcast_in_dim.15), calls=%async_computation.1 | async-start | bytes 2097152 | tf_op jit(solution)/shard_map/all_to_all | solution.py:80
  86.9 13.4 %collective-permute-start.6 = (bf16[2,256,256]{2,1,0:T(8,128)(2,1)}, bf16[2,256,256]{2,1,0:T(8,128)(2,1)}, u32[]{:S(2)}, u32[]{:S(2)}) collective-permute-start(bf16[2,256,256]{2,1,0:T(8,128)(2,1)} %fusion.161), channel_id=1, source_target_pairs={{0,128},{128,0},{1,129},{129,1},{2,130},{130,2},{3,131},{131,3},{4... | collective-permute-start | bytes 786440 | tf_op jit(solution)/shard_map/ppermute | solution.py:99
  92.8 7.6 %collective-permute-start.8 = (bf16[2,256,256]{2,1,0:T(8,128)(2,1)}, bf16[2,256,256]{2,1,0:T(8,128)(2,1)}, u32[]{:S(2)}, u32[]{:S(2)}) collective-permute-start(bf16[2,256,256]{2,1,0:T(8,128)(2,1)} %fusion.160), channel_id=1, source_target_pairs={{0,128},{128,0},{1,129},{129,1},{2,130},{130,2},{3,131},{131,3},{4... | collective-permute-start | bytes 786440 | tf_op jit(solution)/shard_map/ppermute | solution.py:99
  124.5 6.2 %collective-permute-start.9 = (bf16[32,2048]{1,0:T(8,128)(2,1)S(1)}, bf16[32,2048]{1,0:T(8,128)(2,1)S(1)}, u32[]{:S(2)}, u32[]{:S(2)}) collective-permute-start(bf16[32,2048]{1,0:T(8,128)(2,1)S(1)} %convert_element_type.330), channel_id=1, source_target_pairs={{0,16},{16,0},{32,48},{48,32},{1,17},{17,1},{33,49},{49,33},{2,18}... | collective-permute-start | bytes 393224 | tf_op jit(solution)/shard_map/ppermute | solution.py:94
  131.4 7.6 %collective-permute-start.10 = (bf16[32,2048]{1,0:T(8,128)(2,1)}, bf16[32,2048]{1,0:T(8,128)(2,1)}, u32[]{:S(2)}, u32[]{:S(2)}) collective-permute-start(bf16[32,2048]{1,0:T(8,128)(2,1)} %fusion.104), channel_id=1, source_target_pairs={{0,48},{48,0},{16,32},{32,16},{1,49},{49,1},{17,33},{33,17},{2,50}... | collective-permute-start | bytes 393224 | tf_op jit(solution)/shard_map/ppermute | solution.py:94
  156.6 5.3 %collective-permute-start.11 = (bf16[2,256,256]{2,1,0:T(8,128)(2,1)S(1)}, bf16[2,256,256]{2,1,0:T(8,128)(2,1)S(1)}, u32[]{:S(2)}, u32[]{:S(2)}) collective-permute-start(bf16[2,256,256]{2,1,0:T(8,128)(2,1)S(1)} %fusion.159), channel_id=1, source_target_pairs={{0,128},{128,0},{1,129},{129,1},{2,130},{130,2},{3,131},{131,3},{4... | collective-permute-start | bytes 786440 | tf_op jit(solution)/shard_map/ppermute | solution.py:99
  171.6 5.8 %collective-permute-start.12 = (bf16[2,256,256]{2,1,0:T(8,128)(2,1)S(1)}, bf16[2,256,256]{2,1,0:T(8,128)(2,1)S(1)}, u32[]{:S(2)}, u32[]{:S(2)}) collective-permute-start(bf16[2,256,256]{2,1,0:T(8,128)(2,1)S(1)} %fusion.87), channel_id=1, source_target_pairs={{0,128},{128,0},{1,129},{129,1},{2,130},{130,2},{3,131},{131,3},{4... | collective-permute-start | bytes 786440 | tf_op jit(solution)/shard_map/ppermute | solution.py:99
  198.5 6.5 %collective-permute-start.14 = (bf16[32,2048]{1,0:T(8,128)(2,1)S(1)}, bf16[32,2048]{1,0:T(8,128)(2,1)S(1)}, u32[]{:S(2)}, u32[]{:S(2)}) collective-permute-start(bf16[32,2048]{1,0:T(8,128)(2,1)S(1)} %convert_element_type.370), channel_id=1, source_target_pairs={{0,16},{16,0},{32,48},{48,32},{1,17},{17,1},{33,49},{49,33},{2,18}... | collective-permute-start | bytes 393224 | tf_op jit(solution)/shard_map/ppermute | solution.py:94
  205.7 14.9 %collective-permute-start.15 = (bf16[32,2048]{1,0:T(8,128)(2,1)}, bf16[32,2048]{1,0:T(8,128)(2,1)}, u32[]{:S(2)}, u32[]{:S(2)}) collective-permute-start(bf16[32,2048]{1,0:T(8,128)(2,1)} %fusion.105), channel_id=1, source_target_pairs={{0,48},{48,0},{16,32},{32,16},{1,49},{49,1},{17,33},{33,17},{2,50}... | collective-permute-start | bytes 393224 | tf_op jit(solution)/shard_map/ppermute | solution.py:94
  238.5 15.5 %collective-permute-start.17 = (bf16[1024,256]{1,0:T(8,128)(2,1)S(1)}, bf16[1024,256]{1,0:T(8,128)(2,1)S(1)}, u32[]{:S(2)}, u32[]{:S(2)}) collective-permute-start(bf16[1024,256]{1,0:T(8,128)(2,1)S(1)} %slice.248), channel_id=1, source_target_pairs={{0,64},{64,0},{1,65},{65,1},{2,66},{66,2},{3,67},{67,3},{4,68},{68... | collective-permute-start | bytes 1572872 | tf_op jit(solution)/shard_map/ppermute | solution.py:268
  254.2 13.2 %collective-permute-start.18 = (bf16[1024,256]{1,0:T(8,128)(2,1)S(1)}, bf16[1024,256]{1,0:T(8,128)(2,1)S(1)}, u32[]{:S(2)}, u32[]{:S(2)}) collective-permute-start(bf16[1024,256]{1,0:T(8,128)(2,1)S(1)} %add_convert_fusion.2), channel_id=1, source_target_pairs={{0,1},{1,0},{2,3},{3,2},{4,5},{5,4},{6,7},{7,6},{8,9},{9,8},{10,11... | collective-permute-start | bytes 1572872 | tf_op jit(solution)/shard_map/ppermute | solution.py:274
  254.8 7.6 %collective-permute-start.16 = (bf16[2,256,256]{2,1,0:T(8,128)(2,1)S(1)}, bf16[2,256,256]{2,1,0:T(8,128)(2,1)S(1)}, u32[]{:S(2)}, u32[]{:S(2)}) collective-permute-start(bf16[2,256,256]{2,1,0:T(8,128)(2,1)S(1)} %fusion.158), channel_id=1, source_target_pairs={{0,128},{128,0},{1,129},{129,1},{2,130},{130,2},{3,131},{131,3},{4... | collective-permute-start | bytes 786440 | tf_op jit(solution)/shard_map/ppermute | solution.py:99
  276.6 16.0 %collective-permute-start.22 = (bf16[1024,256]{1,0:T(8,128)(2,1)S(1)}, bf16[1024,256]{1,0:T(8,128)(2,1)S(1)}, u32[]{:S(2)}, u32[]{:S(2)}) collective-permute-start(bf16[1024,256]{1,0:T(8,128)(2,1)S(1)} %add_convert_fusion.1), channel_id=1, source_target_pairs={{0,1},{1,0},{2,3},{3,2},{4,5},{5,4},{6,7},{7,6},{8,9},{9,8},{10,11... | collective-permute-start | bytes 1572872 | tf_op jit(solution)/shard_map/ppermute | solution.py:278
  284.8 7.7 %collective-permute-start.21 = (bf16[1024,256]{1,0:T(8,128)(2,1)S(1)}, bf16[1024,256]{1,0:T(8,128)(2,1)S(1)}, u32[]{:S(2)}, u32[]{:S(2)}) collective-permute-start(bf16[1024,256]{1,0:T(8,128)(2,1)S(1)} %slice.256), channel_id=1, source_target_pairs={{0,64},{64,0},{1,65},{65,1},{2,66},{66,2},{3,67},{67,3},{4,68},{68... | collective-permute-start | bytes 1572872 | tf_op jit(solution)/shard_map/ppermute | solution.py:268
  285.0 5.7 %collective-permute-start.25 = (bf16[1024,256]{1,0:T(8,128)(2,1)S(1)}, bf16[1024,256]{1,0:T(8,128)(2,1)S(1)}, u32[]{:S(2)}, u32[]{:S(2)}) collective-permute-start(bf16[1024,256]{1,0:T(8,128)(2,1)S(1)} %slice.260), channel_id=1, source_target_pairs={{0,64},{64,0},{1,65},{65,1},{2,66},{66,2},{3,67},{67,3},{4,68},{68... | collective-permute-start | bytes 1572872 | tf_op jit(solution)/shard_map/ppermute | solution.py:268
  289.5 13.5 %collective-permute-start.24 = (bf16[1024,256]{1,0:T(8,128)(2,1)S(1)}, bf16[1024,256]{1,0:T(8,128)(2,1)S(1)}, u32[]{:S(2)}, u32[]{:S(2)}) collective-permute-start(bf16[1024,256]{1,0:T(8,128)(2,1)S(1)} %add_convert_fusion), channel_id=1, source_target_pairs={{0,1},{1,0},{2,3},{3,2},{4,5},{5,4},{6,7},{7,6},{8,9},{9,8},{10,11... | collective-permute-start | bytes 1572872 | tf_op jit(solution)/shard_map/ppermute | solution.py:281
  (76 other events, 495.0 us)
